TPU v7x, 32 devices: a whole 2x2x4 slice. The times are simulated.
32 devices in a mesh: rep: 4 (over y, x), shard: 8 (over z, core).
Axes of the slice: x: 2, y: 2, z: 4, core: 2. Of those that a mesh axis runs over, the one named last changes fastest.
Arguments:
- tokens: bfloat16 [8192, 1152], P(('rep', 'shard')), may hold values from -6 to 6
- cotangent: bfloat16 [8192, 1152], P(('rep', 'shard')), may hold values from -6 to 6
- lengths: int32 [32, 8], P(('rep', 'shard')), may hold values from 0 to 256, as said below
- deal: int32 [8192], replicated, may hold values from 0 to 8191, as said below
- w_qkv: float32 [1152, 1536], P('shard'), may hold values from -0.3125 to 0.3125
- w_out: float32 [1024, 1152], P('shard'), may hold values from -0.75 to 0.75
- w_gu: float32 [2, 6912, 1152], P(None, 'shard'), may hold values from -0.1875 to 0.1875
- w_down: float32 [6912, 1152], P('shard'), may hold values from -0.078125 to 0.078125
- gains: float32 [4, 1152], P(None, 'shard'), may hold values from 0.5 to 1.5
- first_qkv: float32 [1152, 1536], P('shard'), may hold values from -256 to 256
- first_out: float32 [1024, 1152], P('shard'), may hold values from -128 to 128
- first_gu: float32 [2, 6912, 1152], P(None, 'shard'), may hold values from -256 to 256
- first_down: float32 [6912, 1152], P('shard'), may hold values from -256 to 256
- first_gains: float32 [4, 1152], P(None, 'shard'), may hold values from -512 to 512
- second_qkv: float32 [1152, 1536], P('shard'), may hold values from 2048 to 8192
- second_out: float32 [1024, 1152], P('shard'), may hold values from 512 to 2048
- second_gu: float32 [2, 6912, 1152], P(None, 'shard'), may hold values from 2048 to 8192
- second_down: float32 [6912, 1152], P('shard'), may hold values from 2048 to 8192
- second_gains: float32 [4, 1152], P(None, 'shard'), may hold values from 8192 to 32768
Outputs:
- output: bfloat16 [8192, 1152], P(('rep', 'shard'))
- input_grad: bfloat16 [8192, 1152], P(('rep', 'shard'))
- new_qkv: float32 [1152, 1536], P('shard')
- new_out: float32 [1024, 1152], P('shard')
- new_gu: float32 [2, 6912, 1152], P(None, 'shard')
- new_down: float32 [6912, 1152], P('shard')
- new_gains: float32 [4, 1152], P(None, 'shard')
- moment_qkv: float32 [1152, 1536], P('shard')
- moment_out: float32 [1024, 1152], P('shard')
- moment_gu: float32 [2, 6912, 1152], P(None, 'shard')
- moment_down: float32 [6912, 1152], P('shard')
- moment_gains: float32 [4, 1152], P(None, 'shard')
- square_qkv: float32 [1152, 1536], P('shard')
- square_out: float32 [1024, 1152], P('shard')
- square_gu: float32 [2, 6912, 1152], P(None, 'shard')
- square_down: float32 [6912, 1152], P('shard')
- square_gains: float32 [4, 1152], P(None, 'shard')
- grad_qkv: float32 [1152, 1536], P('shard')
- grad_out: float32 [1024, 1152], P('shard')
- grad_gu: float32 [2, 6912, 1152], P(None, 'shard')
- grad_down: float32 [6912, 1152], P('shard')
- grad_gains: float32 [4, 1152], P(None, 'shard')
- copy_qkv: bfloat16 [1152, 1536], P('shard')
- copy_out: bfloat16 [1024, 1152], P('shard')
- copy_gu: bfloat16 [2, 6912, 1152], P(None, 'shard')
- copy_down: bfloat16 [6912, 1152], P('shard')
- copy_gains: bfloat16 [4, 1152], P(None, 'shard')
Inputs may be any that keep to these rules, and one draw needn't show every extreme that they name: `lengths`: each row sums to 256; in every draw one row holds a single sequence of 256 tokens, the rest zeros. `deal`: a permutation of the slots; each device's input rows go to every device, exactly 8 to each.
All inputs are finite; a program needn't handle non-finite values.
Results may differ from a plain program's by a relative error of at most 0.028.
The roundings to bfloat16 on the way count: a program that leaves them out, or rounds other values in their place, can miss the bound.
Values may be sent and summed in bfloat16 or wider, within the bound.
A program may use at most 384 MiB of HBM per device.

v0:
```python
import functools

import jax
import jax.numpy as jnp
import numpy as np
from jax import lax
from jax.experimental import pallas as pl
from jax.experimental.pallas import tpu as pltpu
from jax.sharding import PartitionSpec as P

H = 4
KV = 1
HD = 256
STEP = 10


CAP_LIMIT = 50.0
NORM_EPS = 1e-06
ROPE_BASE = 10000.0
MASKED_SCORE = -1e30
BETA_FIRST = 0.5
BETA_SECOND = 0.5
ADAM_EPS = 1e-08
LEARN_RATES = (0.05, 0.1, 0.03, 0.012, 0.4)
DECAY_RATES = (0.1, 0.1, 0.1, 0.1, 0.0)
GELU_COEF = 0.7978845608028654
GELU_CUBIC = 0.044715


def rms_scale(values):
    return lax.rsqrt(jnp.mean(values * values, axis=-1, keepdims=True) + NORM_EPS)


def norm_backward(grad_out, values, inverse_rms, gain_row):
    scaled = grad_out * gain_row
    inner = jnp.mean(scaled * values, axis=-1, keepdims=True)
    grad_in = inverse_rms * scaled - values * inverse_rms * inverse_rms * inverse_rms * inner
    grad_gain = jnp.sum(grad_out * values * inverse_rms, axis=0)
    return (grad_in, grad_gain)


def cross_rows(leading, trailing):
    return lax.dot_general(
        leading, trailing, (((0,), (0,)), ((), ())), preferred_element_type=jnp.float32
    )


def against_cols(leading, trailing):
    return lax.dot_general(
        leading, trailing, (((1,), (1,)), ((), ())), preferred_element_type=jnp.float32
    )


def adamw_step(master, gradient, first_moment, second_moment, rate, decay):
    moment = BETA_FIRST * first_moment + (1.0 - BETA_FIRST) * gradient
    square = BETA_SECOND * second_moment + (1.0 - BETA_SECOND) * gradient * gradient
    moment_hat = moment / (1.0 - BETA_FIRST**STEP)
    square_hat = square / (1.0 - BETA_SECOND**STEP)
    updated = master - rate * (moment_hat / (jnp.sqrt(square_hat) + ADAM_EPS) + decay * master)
    return (updated, moment, square)


LANES = 128
UNIT_TILE = 256
MESH = pl.DeviceIdType.MESH


def round_up(count, step):
    return -(-count // step) * step


def partner_of(index, bit):
    value = lax.rem(lax.div(index, 1 << bit), 2)
    return index + (1 - 2 * value) * (1 << bit), value


EARLY = 1


def deal_row(deal_ref, device, rows):
    lines = rows // LANES
    return jnp.concatenate(
        [deal_ref[pl.ds(device * lines + at, 1), :] for at in range(lines)], axis=1
    )


def halving_spans(rep, bits, part, part_rows):
    spans = []
    first = part * part_rows
    size = part_rows
    for bit in range(bits) if part == 0 else range(bits - 1, -1, -1):
        size //= 2
        partner, value = partner_of(rep, bit)
        spans.append((partner, first + value * size, first + (1 - value) * size, size))
        first = first + value * size
    return spans


def at_rows(first, size):
    return pl.ds(pl.multiple_of(first, 16), size)


def feed_kernel(
    line,
    replicas,
    own_rows,
    middle_ref,
    upstream_ref,
    gain_ref,
    weights_hbm,
    out_ref,
    gain_grad_ref,
    back_ref,
    grads_ref,
    weights,
    blocks,
    acts,
    partial,
    chain,
    sibling_out,
    sibling_in,
    landing,
    load_sems,
    store_sems,
    gather_send,
    gather_recv,
    chain_send,
    chain_recv,
    sibling_send,
    sibling_recv,
    half_send,
    half_recv,
):
    rep = lax.axis_index("rep")
    shard = lax.axis_index("shard")
    core = lax.rem(shard, 2)
    place = lax.div(shard, 2)
    sibling = (rep, shard + 1 - 2 * core)
    left = (rep, shard - 2)
    right = (rep, shard + 2)
    has_left = place > 0
    has_right = place < line - 1
    rows = own_rows.shape[0] // 2
    width = own_rows.shape[1]
    half = weights.shape[1] // 2
    tiles = 2 * half // UNIT_TILE

    load = pltpu.make_async_copy(weights_hbm, weights, load_sems.at[0])
    load.start()

    barrier = pltpu.get_barrier_semaphore()
    pl.semaphore_signal(barrier, inc=1, device_id=sibling, device_id_type=MESH)

    @pl.when(has_left)
    def _():
        pl.semaphore_signal(barrier, inc=1, device_id=left, device_id_type=MESH)

    @pl.when(has_right)
    def _():
        pl.semaphore_signal(barrier, inc=1, device_id=right, device_id_type=MESH)

    bits = replicas.bit_length() - 1
    greeted = sorted({0, bits - 1})
    for bit in greeted:
        partner, _ = partner_of(rep, bit)
        pl.semaphore_signal(barrier, inc=1, device_id=(partner, shard), device_id_type=MESH)

    def block_span(block):
        return pl.ds(pl.multiple_of(block * rows, rows), rows)

    for part in range(2):
        blocks[0, part, block_span(place), :] = own_rows[part * rows : (part + 1) * rows, :]

    pl.semaphore_wait(
        barrier,
        1 + len(greeted) + has_left.astype(jnp.int32) + has_right.astype(jnp.int32),
    )

    def gather_copy(phase, part, way, step, block):
        return pltpu.make_async_remote_copy(
            src_ref=blocks.at[phase, part, block_span(block)],
            dst_ref=blocks.at[phase, part, block_span(block)],
            send_sem=gather_send.at[phase, part, way, step],
            recv_sem=gather_recv.at[phase, part, way, step],
            device_id=left if way else right,
            device_id_type=MESH,
        )

    def gather_start(phase, part, step):
        @pl.when(has_right & (place - step >= 0))
        def _():
            gather_copy(phase, part, 0, step, place - step).start()

        @pl.when(has_left & (place + step <= line - 1))
        def _():
            gather_copy(phase, part, 1, step, place + step).start()

    def gather_arrive(phase, part, step):
        @pl.when(place - 1 - step >= 0)
        def _():
            gather_copy(phase, part, 0, step, place - 1 - step).wait_recv()

        @pl.when(place + 1 + step <= line - 1)
        def _():
            gather_copy(phase, part, 1, step, place + 1 + step).wait_recv()

    def gather_drain(phase, part):
        @pl.loop(0, line - 1)
        def _(step):
            @pl.when(has_right & (place - step >= 0))
            def _():
                gather_copy(phase, part, 0, step, place - step).wait_send()

            @pl.when(has_left & (place + step <= line - 1))
            def _():
                gather_copy(phase, part, 1, step, place + step).wait_send()

    def chain_copy(phase, part, way, packet, block):
        return pltpu.make_async_remote_copy(
            src_ref=partial.at[part, block_span(block)],
            dst_ref=chain.at[part, way, packet],
            send_sem=chain_send.at[phase, part, way, packet],
            recv_sem=chain_recv.at[phase, part, way, packet],
            device_id=left if way else right,
            device_id_type=MESH,
        )

    def chain_add(phase, part, way, packet, block):
        chain_copy(phase, part, way, packet, block).wait_recv()
        span = block_span(block)
        partial[part, span, :] = (
            partial[part, span, :].astype(jnp.float32) + chain[part, way, packet].astype(jnp.float32)
        ).astype(partial.dtype)

    def chain_turn(phase, part, turn):
        outward = turn - place

        @pl.when(outward >= 0)
        def _():
            @pl.when(has_left)
            def _():
                chain_add(phase, part, 0, outward, line - 1 - outward)

            chain_copy(phase, part, 0, outward, line - 1 - outward).start()

        inward = turn - (line - 1 - place)

        @pl.when(inward >= 0)
        def _():
            @pl.when(has_right)
            def _():
                chain_add(phase, part, 1, inward, inward)

            chain_copy(phase, part, 1, inward, inward).start()

    def chain_finish(phase, part):
        out = slice(part * rows, (part + 1) * rows)
        back_ref[out, :] = partial[part, block_span(place), :].astype(jnp.float32)

        @pl.when(has_left)
        def _():
            last = line - 1 - place
            chain_copy(phase, part, 0, last, place).wait_recv()
            back_ref[out, :] += chain[part, 0, last].astype(jnp.float32)

        @pl.when(has_right)
        def _():
            chain_copy(phase, part, 1, place, place).wait_recv()
            back_ref[out, :] += chain[part, 1, place].astype(jnp.float32)

    def chain_drain(phase, part):
        @pl.loop(0, line - 1)
        def _(packet):
            @pl.when(line - 1 - packet > place)
            def _():
                chain_copy(phase, part, 0, packet, line - 1 - packet).wait_send()

            @pl.when(packet < place)
            def _():
                chain_copy(phase, part, 1, packet, packet).wait_send()

    def sweep(phase, part, work, reduce=None, last=None, beside=None):
        @pl.loop(1, line)
        def _(turn):
            gather_arrive(phase, part, turn - 1)

            @pl.when(turn < line - 1)
            def _():
                gather_start(phase, part, turn)
                if reduce is not None:
                    chain_turn(*reduce, turn)

            if last is not None:

                @pl.when(turn == line - 1)
                def _():
                    last()

            @pl.loop(0, line // 2)
            def _(pair):
                ready = jnp.maximum(jnp.abs(2 * pair - place), jnp.abs(2 * pair + 1 - place))

                @pl.when(ready == turn)
                def _():
                    work(part, pair)

            if beside is not None:
                beside(turn)

    def pair_span(pair):
        return pl.ds(pl.multiple_of(pair * 2 * rows, 2 * rows), 2 * rows)

    def token_span(part, pair):
        first = part * line * rows
        return pl.ds(pl.multiple_of(first + pair * 2 * rows, 2 * rows), 2 * rows)

    def unit_span(tile):
        return pl.ds(pl.multiple_of(tile * UNIT_TILE, UNIT_TILE), UNIT_TILE)

    def forward(part, pair):
        span = token_span(part, pair)

        @pl.loop(0, tiles)
        def _(tile):
            cols = unit_span(tile)
            rows_in = blocks[0, part, pair_span(pair), :]
            gate = against_cols(rows_in, weights[1, cols, :])
            upper = against_cols(rows_in, weights[2, cols, :])
            tanh_inner = jnp.tanh(GELU_COEF * (gate + GELU_CUBIC * gate * gate * gate))
            lifted = 0.5 * (1.0 + tanh_inner)
            activated = gate * lifted
            slope = lifted + 0.5 * gate * (1.0 - tanh_inner * tanh_inner) * GELU_COEF * (
                1.0 + 3.0 * GELU_CUBIC * gate * gate
            )
            acts[0, span, cols] = (activated * upper).astype(acts.dtype)
            acts[1, span, cols] = (upper * slope).astype(acts.dtype)
            acts[2, span, cols] = activated.astype(acts.dtype)

        partial[part, pair_span(pair), :] = jnp.dot(
            acts[0, span, :], weights[0], preferred_element_type=jnp.float32
        ).astype(partial.dtype)

    def backward(part, pair):
        span = token_span(part, pair)

        @pl.loop(0, tiles)
        def _(tile):
            cols = unit_span(tile)
            grad_hidden = against_cols(blocks[1, part, pair_span(pair), :], weights[0, cols, :])
            for member in (1, 2):
                acts[member, span, cols] = (
                    grad_hidden * acts[member, span, cols].astype(jnp.float32)
                ).astype(acts.dtype)

        partial[part, pair_span(pair), :] = (
            jnp.dot(acts[1, span, :], weights[1], preferred_element_type=jnp.float32)
            + jnp.dot(acts[2, span, :], weights[2], preferred_element_type=jnp.float32)
        ).astype(partial.dtype)

    def output_half(part):
        out = slice(part * rows, (part + 1) * rows)
        feed = back_ref[out, :]
        upstream = upstream_ref[out, :].astype(jnp.float32)
        gain = gain_ref[3:4, :]
        inverse = lax.rsqrt(jnp.mean(feed * feed, axis=-1, keepdims=True) + NORM_EPS)
        scaled = upstream * gain
        inner = jnp.mean(scaled * feed, axis=-1, keepdims=True)
        blocks[1, part, block_span(place), :] = (
            inverse * scaled - feed * inverse * inverse * inverse * inner
        ).astype(blocks.dtype)
        gather_start(1, part, 0)
        gain_grad = jnp.sum(upstream * feed * inverse, axis=0, keepdims=True)
        if part == 0:
            gain_grad_ref[...] = gain_grad
        else:
            gain_grad_ref[...] += gain_grad
        out_ref[out, :] = (middle_ref[out, :] + feed * inverse * gain).astype(out_ref.dtype)

    def sibling_copy(member):
        return pltpu.make_async_remote_copy(
            src_ref=sibling_out.at[member],
            dst_ref=sibling_in.at[member],
            send_sem=sibling_send.at[member],
            recv_sem=sibling_recv.at[member],
            device_id=sibling,
            device_id_type=MESH,
        )

    def store_copy(member):
        return pltpu.make_async_copy(
            sibling_in.at[member], grads_ref.at[member], store_sems.at[member]
        )

    cuts = [(start, min(512, half - start)) for start in range(0, half, 512)]

    def far_grad(part, member):
        tokens = line * rows
        trailing = jnp.where(member == 0, 1, 0)
        for start, size in cuts:
            span = slice(start, start + size)
            piece = cross_rows(
                acts[member, part * tokens : (part + 1) * tokens, half + start : half + start + size],
                blocks[trailing, part],
            )
            if part == 1:
                piece = piece + sibling_out[member, span, :].astype(jnp.float32)
            sibling_out[member, span, :] = piece.astype(sibling_out.dtype)
        if part == 1:
            sibling_copy(member).start()

    first_spans = [halving_spans(rep, bits, part, half // 2)[0] for part in range(2)]

    def halve(member, part):
        partner, keep, give, size = first_spans[part]
        return pltpu.make_async_remote_copy(
            src_ref=sibling_in.at[member, at_rows(give, size)],
            dst_ref=landing.at[member, part],
            send_sem=half_send.at[member, part],
            recv_sem=half_recv.at[member, part],
            device_id=(partner, shard),
            device_id_type=MESH,
        )

    def near_grad(member):
        trailing = jnp.where(member == 0, 1, 0)
        sibling_copy(member).wait_recv()
        for start, size in cuts:
            span = slice(start, start + size)
            piece = cross_rows(
                acts[member, :, span], blocks[trailing].reshape(2 * line * rows, width)
            )
            sibling_in[member, span, :] = (
                sibling_in[member, span, :].astype(jnp.float32) + piece
            ).astype(sibling_in.dtype)

        @pl.when(member < EARLY)
        def _():
            for part in range(2):
                halve(member, part).start()

        @pl.when(member >= EARLY)
        def _():
            store_copy(member).start()

    def share(turn, count, turns):
        return lax.div(turn * count, turns), lax.div((turn + 1) * count, turns)

    def first_grads(turn):
        @pl.when(turn < line - 1)
        def _():
            @pl.loop(*share(turn - 1, 3, line - 2))
            def _(member):
                far_grad(0, member)

    def last_grads(turn):
        @pl.loop(*share(turn, 6, line - 1))
        def _(unit):
            @pl.when(unit < 3)
            def _():
                far_grad(1, unit)

            @pl.when(unit >= 3)
            def _():
                near_grad(unit - 3)

    def turn_around(part):
        chain_finish(0, part)
        output_half(part)

    gather_start(0, 0, 0)
    load.wait()
    sweep(0, 0, forward, last=lambda: gather_start(0, 1, 0))
    chain_turn(0, 0, 0)
    sweep(0, 1, forward, reduce=(0, 0), last=lambda: turn_around(0))
    chain_turn(0, 1, 0)
    chain_drain(0, 0)
    sweep(1, 0, backward, reduce=(0, 1), last=lambda: turn_around(1))
    chain_turn(1, 0, 0)
    chain_drain(0, 1)
    sweep(1, 1, backward, reduce=(1, 0), beside=first_grads)
    chain_turn(1, 1, 0)
    chain_finish(1, 0)

    @pl.loop(0, line - 1)
    def _(turn):
        @pl.when(turn > 0)
        def _():
            chain_turn(1, 1, turn)

        last_grads(turn)

    chain_finish(1, 1)
    for member in range(EARLY):
        for part in range(2):
            halve(member, part).wait_recv()
            partner, keep, give, size = first_spans[part]
            kept = at_rows(keep, size)
            sibling_in[member, kept, :] = (
                sibling_in[member, kept, :].astype(jnp.float32)
                + landing[member, part].astype(jnp.float32)
            ).astype(sibling_in.dtype)
        store_copy(member).start()
    for part in range(2):
        for phase in range(2):
            gather_drain(phase, part)
        chain_drain(1, part)
        for member in range(EARLY):
            halve(member, part).wait_send()
    for member in range(3):
        sibling_copy(member).wait_send()
        store_copy(member).wait()


def feed_forward(line, replicas, normed, middle, upstream, gains, weights):
    rows, width = normed.shape
    half = weights.shape[1] // 2
    low = jnp.bfloat16
    full = jnp.float32
    vmem = pl.BlockSpec(memory_space=pltpu.VMEM)
    hbm = pl.BlockSpec(memory_space=pl.ANY)
    tokens = line * rows
    return pl.pallas_call(
        functools.partial(feed_kernel, line, replicas),
        out_shape=(
            jax.ShapeDtypeStruct((rows, width), low),
            jax.ShapeDtypeStruct((1, width), full),
            jax.ShapeDtypeStruct((rows, width), full),
            jax.ShapeDtypeStruct((3, half, width), low),
        ),
        in_specs=[vmem, vmem, vmem, vmem, hbm],
        out_specs=(vmem, vmem, vmem, hbm),
        scratch_shapes=[
            pltpu.VMEM((3, 2 * half, width), low),
            pltpu.VMEM((2, 2, tokens // 2, width), low),
            pltpu.VMEM((3, tokens, 2 * half), low),
            pltpu.VMEM((2, tokens // 2, width), low),
            pltpu.VMEM((2, 2, line - 1, rows // 2, width), low),
            pltpu.VMEM((3, half, width), low),
            pltpu.VMEM((3, half, width), low),
            pltpu.VMEM((EARLY, 2, half // 4, width), low),
            pltpu.SemaphoreType.DMA((1,)),
            pltpu.SemaphoreType.DMA((3,)),
            pltpu.SemaphoreType.DMA((2, 2, 2, line - 1)),
            pltpu.SemaphoreType.DMA((2, 2, 2, line - 1)),
            pltpu.SemaphoreType.DMA((2, 2, 2, line - 1)),
            pltpu.SemaphoreType.DMA((2, 2, 2, line - 1)),
            pltpu.SemaphoreType.DMA((3,)),
            pltpu.SemaphoreType.DMA((3,)),
            pltpu.SemaphoreType.DMA((EARLY, 2)),
            pltpu.SemaphoreType.DMA((EARLY, 2)),
        ],
        compiler_params=pltpu.CompilerParams(
            collective_id=0, has_side_effects=True, vmem_limit_bytes=63 * 1024 * 1024
        ),
        cost_estimate=pl.CostEstimate(
            flops=18 * tokens * 2 * half * width,
            bytes_accessed=9 * half * width * 2,
            transcendentals=tokens * 2 * half,
        ),
    )(normed, middle, upstream, gains, weights)


def back_kernel(
    line,
    replicas,
    back_hbm,
    middle_hbm,
    upstream_hbm,
    branch_hbm,
    inputs_hbm,
    normed_hbm,
    attended_hbm,
    queries_hbm,
    keys_hbm,
    values_hbm,
    cosine_hbm,
    sine_hbm,
    doc_col_ref,
    doc_row_ref,
    gains_ref,
    last_gain_ref,
    out_rows_ref,
    deal_ref,
    first_hbm,
    out_hbm,
    grads_hbm,
    first_half_hbm,
    second_half_hbm,
    qkv_hbm,
    outw_hbm,
    output_ref,
    input_grad_ref,
    w_qkv,
    w_out,
    acc,
    total,
    landing,
    late_landing,
    query_parts,
    query_pair,
    query_chain,
    query_steps,
    query_land,
    key_parts,
    key_pair,
    key_chain,
    key_steps,
    key_land,
    out_parts,
    out_pair,
    out_chain,
    out_steps,
    out_land,
    grad_rows,
    grad_keys,
    grad_values,
    pack_rows,
    send_rows,
    recv_rows,
    held,
    operand_sems,
    load_sems,
    store_sems,
    half_send,
    half_recv,
    pair_send,
    pair_recv,
    chain_send,
    chain_recv,
    step_send,
    step_recv,
    row_send,
    row_recv,
):
    rep = lax.axis_index("rep")
    shard = lax.axis_index("shard")
    shards = 2 * line
    devices = replicas * shards
    me = rep * shards + shard
    core = lax.rem(shard, 2)
    place = lax.div(shard, 2)
    sibling = (rep, shard + 1 - 2 * core)
    left = (rep, shard - 2)
    right = (rep, shard + 2)
    has_left = place > 0
    has_right = place < line - 1
    bits = replicas.bit_length() - 1
    full = jnp.float32
    rows, width = inputs_hbm.shape
    key_width = keys_hbm.shape[1]
    query_width = queries_hbm.shape[1]
    heads = query_width // key_width
    members, half_rows = acc.shape[0], acc.shape[1]
    part_rows = half_rows // 2
    peer_rows = rows // devices
    block_rows = send_rows.shape[2]
    packed = devices * block_rows
    qkv_rows = first_hbm.shape[0] // shards
    out_rows = out_hbm.shape[0] // shards

    load_qkv = pltpu.make_async_copy(first_hbm, w_qkv, load_sems.at[0])
    load_out = pltpu.make_async_copy(out_hbm, w_out, load_sems.at[1])
    load_acc = pltpu.make_async_copy(grads_hbm, acc, load_sems.at[2])
    operands = (
        back_hbm,
        middle_hbm,
        upstream_hbm,
        branch_hbm,
        inputs_hbm,
        normed_hbm,
        attended_hbm,
        queries_hbm,
        keys_hbm,
        values_hbm,
        cosine_hbm,
        sine_hbm,
    )
    operand_loads = [
        pltpu.make_async_copy(source, target, operand_sems.at[at])
        for at, (source, target) in enumerate(zip(operands, held))
    ]
    (
        back_ref,
        middle_ref,
        upstream_ref,
        branch_ref,
        inputs_ref,
        normed_ref,
        attended_ref,
        queries_ref,
        keys_ref,
        values_ref,
        cosine_ref,
        sine_ref,
    ) = held
    load_acc.start()
    for load in operand_loads:
        load.start()
    load_out.start()
    load_qkv.start()

    barrier = pltpu.get_barrier_semaphore()

    @pl.loop(1, devices)
    def _(hop):
        peer = lax.rem(me + hop, devices)
        pl.semaphore_signal(
            barrier,
            inc=1,
            device_id=(lax.div(peer, shards), lax.rem(peer, shards)),
            device_id_type=MESH,
        )

    pl.semaphore_wait(barrier, devices - 1)

    spans = [halving_spans(rep, bits, part, part_rows) for part in range(2)]

    def first_stage(member):
        return 1 if member < EARLY else 0

    def landed(member, part, stage):
        if stage == 0:
            return landing.at[member - EARLY, part]
        size = part_rows >> (stage + 1)
        return late_landing.at[member, part, pl.ds(part_rows // 2 - 2 * size, size)]

    def halve(member, part, stage):
        partner, keep, give, size = spans[part][stage]
        source = grads_hbm if stage == first_stage(member) else acc
        return pltpu.make_async_remote_copy(
            src_ref=source.at[member, at_rows(give, size)],
            dst_ref=landed(member, part, stage),
            send_sem=half_send.at[0, member, part, stage],
            recv_sem=half_recv.at[0, member, part, stage],
            device_id=(partner, shard),
            device_id_type=MESH,
        )

    def halve_add(member, part, stage):
        partner, keep, give, size = spans[part][stage]
        halve(member, part, stage).wait_recv()
        target = total if stage == bits - 1 else acc
        target[member, at_rows(keep, size), :] = (
            acc[member, at_rows(keep, size), :].astype(full)
            + landed(member, part, stage)[...].astype(full)
        ).astype(acc.dtype)

    def double(member, part, stage):
        partner, keep, give, size = spans[part][stage]
        return pltpu.make_async_remote_copy(
            src_ref=total.at[member, at_rows(keep, size)],
            dst_ref=total.at[member, at_rows(keep, size)],
            send_sem=half_send.at[1, member, part, stage],
            recv_sem=half_recv.at[1, member, part, stage],
            device_id=(partner, shard),
            device_id_type=MESH,
        )

    def double_arrive(member, part, stage):
        partner, keep, give, size = spans[part][stage]
        pltpu.make_async_remote_copy(
            src_ref=total.at[member, at_rows(give, size)],
            dst_ref=total.at[member, at_rows(give, size)],
            send_sem=half_send.at[1, member, part, stage],
            recv_sem=half_recv.at[1, member, part, stage],
            device_id=(partner, shard),
            device_id_type=MESH,
        ).wait_recv()

    def each(work):
        for member in range(members):
            for part in range(2):
                work(member, part)

    for part in range(2):
        halve(members - 1, part, first_stage(members - 1)).start()
    for member in range(members - 1):
        for part in range(2):
            halve(member, part, first_stage(member)).start()
    load_acc.wait()

    def pair_copy(kind, parts, pair):
        return pltpu.make_async_remote_copy(
            src_ref=parts.at[1 - core],
            dst_ref=pair,
            send_sem=pair_send.at[kind],
            recv_sem=pair_recv.at[kind],
            device_id=sibling,
            device_id_type=MESH,
        )

    kinds = (
        (out_parts, out_pair, out_chain, out_steps, out_land),
        (query_parts, query_pair, query_chain, query_steps, query_land),
        (key_parts, key_pair, key_chain, key_steps, key_land),
    )

    def pair_add(kind):
        parts, pair = kinds[kind][:2]
        pair_copy(kind, parts, pair).wait_recv()

        @pl.loop(0, line)
        def _(block):
            parts[core, block] = (
                parts[core, block].astype(full) + pair[block].astype(full)
            ).astype(parts.dtype)

    def chain_copy(kind, way, step, block):
        parts, _, chain = kinds[kind][:3]
        return pltpu.make_async_remote_copy(
            src_ref=parts.at[core, block],
            dst_ref=chain.at[way, step],
            send_sem=chain_send.at[kind, way, step],
            recv_sem=chain_recv.at[kind, way, step],
            device_id=left if way else right,
            device_id_type=MESH,
        )

    def chain_add(kind, way, step, block):
        parts, _, chain = kinds[kind][:3]
        chain_copy(kind, way, step, block).wait_recv()
        parts[core, block] = (
            parts[core, block].astype(full) + chain[way, step].astype(full)
        ).astype(parts.dtype)

    def chain_step(kind, turn):
        outward = turn - place

        @pl.when(outward >= 0)
        def _():
            @pl.when(has_left)
            def _():
                chain_add(kind, 0, outward, line - 1 - outward)

            chain_copy(kind, 0, outward, line - 1 - outward).start()

        inward = turn - (line - 1 - place)

        @pl.when(inward >= 0)
        def _():
            @pl.when(has_right)
            def _():
                chain_add(kind, 1, inward, inward)

            chain_copy(kind, 1, inward, inward).start()

    def chain_finish(kind):
        parts, _, _, steps, _ = kinds[kind]

        @pl.when(has_left)
        def _():
            chain_add(kind, 0, line - 1 - place, place)

        @pl.when(has_right)
        def _():
            chain_add(kind, 1, place, place)

        steps[0] = parts[core, place]

    lanes = {0: ((0, None),), 1: ((1, 0), (2, 1)), 2: ((3, None),)}

    def columns(ref, piece):
        if piece is None:
            return ref
        size = ref.shape[1] // 2
        return ref.at[:, pl.ds(piece * size, size)]

    def step_copy(kind, stage, lane, piece):
        steps, land = kinds[kind][3:]
        partner, _ = partner_of(rep, stage if lane in (1, 3) else bits - 1 - stage)
        return pltpu.make_async_remote_copy(
            src_ref=columns(steps.at[stage], piece),
            dst_ref=columns(land.at[stage], piece),
            send_sem=step_send.at[lane, stage],
            recv_sem=step_recv.at[lane, stage],
            device_id=(partner, shard),
            device_id_type=MESH,
        )

    def step_start(kind, stage):
        for lane, piece in lanes[kind]:
            step_copy(kind, stage, lane, piece).start()

    def step_add(kind, stage):
        steps, land = kinds[kind][3:]
        for lane, piece in lanes[kind]:
            step_copy(kind, stage, lane, piece).wait_recv()
            columns(steps.at[stage + 1], piece)[...] = (
                columns(steps.at[stage], piece)[...].astype(full)
                + columns(land.at[stage], piece)[...].astype(full)
            ).astype(steps.dtype)
            if stage + 1 < bits:
                step_copy(kind, stage + 1, lane, piece).start()

    served = {0: 0}

    def chain_to(kind, end):
        for step in range(served[kind], end):
            chain_step(kind, step)
        served[kind] = max(end, served[kind])

    def advance(member, stage):
        for part in range(2):
            halve_add(member, part, stage)
            if stage + 1 < bits:
                halve(member, part, stage + 1).start()
            else:
                double(member, part, stage).start()

    def redouble(member, stage):
        for part in range(2):
            double_arrive(member, part, stage)
            if stage > 1:
                double(member, part, stage - 1).start()
            else:
                store_half(member, part).start()

    def store_half(member, part):
        _, keep, _, size = spans[part][0]
        return pltpu.make_async_copy(
            total.at[member, at_rows(keep, size)],
            (first_half_hbm, second_half_hbm)[part].at[member],
            store_sems.at[3 + 2 * member + part],
        )

    todo = [
        [functools.partial(advance, member, stage) for stage in range(first_stage(member), bits)]
        + [functools.partial(redouble, member, stage) for stage in range(bits - 1, 0, -1)]
        for member in range(members)
    ]

    def serve(*chosen):
        for member in chosen:
            if todo[member]:
                todo[member].pop(0)()

    for load in operand_loads:
        load.wait()
    middle = middle_ref[...]
    upstream = upstream_ref[...].astype(full)
    scale_two = rms_scale(middle)
    grad_middle_norm, gain_two = norm_backward(
        back_ref[...], middle, scale_two, gains_ref[2:3, :]
    )
    back_ref[...] = upstream + grad_middle_norm
    branch = branch_ref[...]
    grad_branch, gain_one = norm_backward(
        back_ref[...], branch, rms_scale(branch), gains_ref[1:2, :]
    )
    grad_branch = grad_branch.astype(jnp.bfloat16)
    half_query = query_width // 2
    half_shards = shards // 2
    for group in range(2):
        grad_out = cross_rows(
            attended_ref[:, group * half_query : (group + 1) * half_query], grad_branch
        )
        for offset in range(half_shards):
            member = group * half_shards + offset
            out_parts[member % 2, member // 2, 0:out_rows, :] = grad_out[
                offset * out_rows : (offset + 1) * out_rows
            ].astype(out_parts.dtype)

    pair_copy(0, out_parts, out_pair).start()
    load_out.wait()
    grad_rows[:, 0:query_width] = against_cols(grad_branch, w_out[...]).astype(grad_rows.dtype)
    grad_keys[...] = jnp.zeros_like(grad_keys)
    grad_values[...] = jnp.zeros_like(grad_values)
    half_key = key_width // 2

    down_ids = lax.broadcasted_iota(jnp.int32, (rows, rows), 0)
    along_ids = lax.broadcasted_iota(jnp.int32, (rows, rows), 1)
    own_slots = down_ids + me * rows

    def find(source, found):
        return found + jnp.where(deal_row(deal_ref, source, rows) == own_slots, source, 0)

    found = lax.fori_loop(0, devices, find, jnp.zeros((rows, rows), jnp.int32))
    origin = jnp.sum(found, axis=1, keepdims=True)
    origin_row = jnp.sum(jnp.where(down_ids == along_ids, origin, 0), axis=0, keepdims=True)
    before = (origin_row == origin) & (down_ids < along_ids)
    back_place = origin_row * block_rows + jnp.sum(
        before.astype(jnp.int32), axis=0, keepdims=True
    )
    pack_rows[...] = (
        lax.broadcasted_iota(jnp.int32, (packed, rows), 0) == back_place
    ).astype(pack_rows.dtype)

    def row_copy(kind, hop, peer, source):
        return pltpu.make_async_remote_copy(
            src_ref=send_rows.at[kind, peer],
            dst_ref=recv_rows.at[kind, source],
            send_sem=row_send.at[kind, hop],
            recv_sem=row_recv.at[kind, hop],
            device_id=(lax.div(peer, shards), lax.rem(peer, shards)),
            device_id_type=MESH,
        )

    def send_back(kind, values):
        send_rows[kind] = (
            jnp.dot(pack_rows[...], values, preferred_element_type=full)
            .reshape(devices, block_rows, width)
            .astype(send_rows.dtype)
        )
        recv_rows[kind, me] = send_rows[kind, me]

        @pl.loop(1, devices)
        def _(hop):
            row_copy(kind, hop, lax.rem(me + hop, devices), me).start()

    send_back(0, out_rows_ref[...])
    pair_add(0)
    chain_to(0, 1)

    for head in range(heads):
        start = head * key_width
        cols = pl.ds(start, key_width)
        query = queries_ref[:, cols]
        key = keys_ref[...]
        allowed = (doc_col_ref[...] == doc_row_ref[...]) & (
            lax.broadcasted_iota(jnp.int32, (rows, rows), 0)
            >= lax.broadcasted_iota(jnp.int32, (rows, rows), 1)
        )
        tanh_scores = jnp.tanh(against_cols(query, key) * (HD ** (-0.5) / CAP_LIMIT))
        capped = jnp.where(allowed, CAP_LIMIT * tanh_scores, MASKED_SCORE)
        powers = jnp.exp(capped - jnp.max(capped, axis=-1, keepdims=True))
        probs = powers / jnp.sum(powers, axis=-1, keepdims=True)
        grad_att = grad_rows[:, cols]
        grad_values[...] += cross_rows(probs.astype(jnp.bfloat16), grad_att)
        grad_probs = against_cols(grad_att, values_ref[...])
        grad_capped = probs * (grad_probs - jnp.sum(probs * grad_probs, axis=-1, keepdims=True))
        grad_raw = (
            grad_capped * (1.0 - tanh_scores * tanh_scores) * HD ** (-0.5)
        ).astype(jnp.bfloat16)
        grad_keys[...] += cross_rows(grad_raw, query)
        grad_query = jnp.dot(grad_raw, key, preferred_element_type=full)
        front = grad_query[:, :half_key]
        back = grad_query[:, half_key:]
        cosine, sine = cosine_ref[...], sine_ref[...]
        grad_rows[:, pl.ds(start, half_key)] = (front * cosine + back * sine).astype(
            grad_rows.dtype
        )
        grad_rows[:, pl.ds(start + half_key, half_key)] = (
            back * cosine - front * sine
        ).astype(grad_rows.dtype)

    def weight_parts(parts, first, size):
        for begin in range(0, size, 512):
            grad_cols = cross_rows(
                normed_ref[...], grad_rows[:, first + begin : first + begin + 512]
            )
            for member in range(shards):
                parts[member % 2, member // 2, 0:qkv_rows, begin : begin + 512] = grad_cols[
                    member * qkv_rows : (member + 1) * qkv_rows
                ].astype(parts.dtype)

    weight_parts(query_parts, 0, query_width)
    pair_copy(1, query_parts, query_pair).start()
    serve(members - 1, 0)
    chain_to(0, min(2, line - 1))
    front = grad_keys[:, :half_key]
    back = grad_keys[:, half_key:]
    cosine, sine = cosine_ref[...], sine_ref[...]
    grad_rows[:, query_width : query_width + half_key] = (
        front * cosine + back * sine
    ).astype(grad_rows.dtype)
    grad_rows[:, query_width + half_key : query_width + key_width] = (
        back * cosine - front * sine
    ).astype(grad_rows.dtype)
    grad_rows[:, query_width + key_width :] = grad_values[...].astype(grad_rows.dtype)
    pair_add(1)
    chain_step(1, 0)

    load_qkv.wait()
    grad_normed = against_cols(grad_rows[...], w_qkv[...])
    inputs = inputs_ref[...].astype(full)
    grad_norm, gain_zero = norm_backward(
        grad_normed, inputs, rms_scale(inputs), gains_ref[0:1, :]
    )
    grad_inputs = (back_ref[...] + grad_norm).astype(jnp.bfloat16)
    weight_parts(key_parts, query_width, 2 * key_width)
    gain_stack = jnp.stack([gain_zero, gain_one, gain_two, last_gain_ref[0]])
    third = width // 3
    gain_rows = jnp.concatenate(
        [gain_stack[:, at * third : (at + 1) * third] for at in range(3)]
        + [jnp.zeros((4, third), full)]
    ).astype(jnp.bfloat16)
    for member in range(shards):
        gain_at = key_parts.shape[2] - 16
        key_parts[member % 2, member // 2, gain_at:, 0:third] = gain_rows
        key_parts[member % 2, member // 2, gain_at:, third:] = jnp.zeros(
            (16, key_parts.shape[3] - third), key_parts.dtype
        )
    pair_copy(2, key_parts, key_pair).start()
    serve(1)

    if line > 2:
        chain_step(1, 1)
    pair_add(2)
    chain_step(2, 0)
    chain_to(0, line - 1)
    chain_finish(0)
    step_start(0, 0)
    serve(members - 1, 0)
    for step in range(2, line - 1):
        chain_step(1, step)
        chain_step(2, step - 1)
    if line > 2:
        chain_step(2, line - 2)
    chain_finish(1)
    step_start(1, 0)
    send_back(1, grad_inputs)
    serve(1, members - 1)
    step_add(0, 0)
    serve(0)
    chain_finish(2)
    step_start(2, 0)
    for stage in range(1, bits):
        step_add(0, stage)
    for stage in range(bits):
        serve(*range(members))
        for kind in (1, 2):
            step_add(kind, stage)
    while any(todo):
        serve(*range(members))
    store_small = (
        pltpu.make_async_copy(out_steps.at[bits], outw_hbm, store_sems.at[0]),
        pltpu.make_async_copy(
            query_steps.at[bits],
            qkv_hbm.at[pl.ds(0, query_steps.shape[1]), pl.ds(0, query_width)],
            store_sems.at[1],
        ),
        pltpu.make_async_copy(
            key_steps.at[bits], qkv_hbm.at[:, pl.ds(query_width, 2 * key_width)], store_sems.at[2]
        ),
    )
    for store in store_small:
        store.start()
    own_deal = deal_row(deal_ref, me, rows)
    own_column = jnp.sum(jnp.where(down_ids == along_ids, own_deal, 0), axis=1, keepdims=True)
    send_place = jnp.sum((own_deal < own_column).astype(jnp.int32), axis=1, keepdims=True)
    target = lax.div(send_place, peer_rows) * block_rows + lax.rem(send_place, peer_rows)
    placer = (
        lax.broadcasted_iota(jnp.int32, (rows, packed), 1) == target
    ).astype(jnp.bfloat16)
    for kind, result in enumerate((output_ref, input_grad_ref)):

        @pl.loop(1, devices)
        def _(hop, kind=kind):
            source = lax.rem(me + devices - hop, devices)
            row_copy(kind, hop, source, source).wait_recv()

        stacked = recv_rows[kind].astype(full).reshape(packed, width).astype(jnp.bfloat16)
        result[...] = jnp.dot(placer, stacked, preferred_element_type=full).astype(result.dtype)

    for kind in range(2):

        @pl.loop(1, devices)
        def _(hop, kind=kind):
            row_copy(kind, hop, lax.rem(me + hop, devices), me).wait_send()

    def sent(member, part):
        for stage in range(bits):
            if stage >= first_stage(member):
                halve(member, part, stage).wait_send()
            if stage > 0:
                double(member, part, stage).wait_send()

    each(sent)
    for kind in range(3):
        parts, pair = kinds[kind][:2]
        pair_copy(kind, parts, pair).wait_send()
        for stage in range(bits):
            for lane, piece in lanes[kind]:
                step_copy(kind, stage, lane, piece).wait_send()

        @pl.loop(0, line - 1)
        def _(step, kind=kind):
            far = line - 1 - step

            @pl.when(far > place)
            def _():
                chain_copy(kind, 0, step, far).wait_send()

            @pl.when(step < place)
            def _():
                chain_copy(kind, 1, step, step).wait_send()

    for store in store_small:
        store.wait()
    each(lambda member, part: store_half(member, part).wait())


def back_and_reduce(line, replicas, small, first_full, out_full, ff_grads):
    inputs, normed, queries, keys = small[4], small[5], small[7], small[8]
    held = 12
    rows, width = inputs.shape
    shards = 2 * line
    devices = replicas * shards
    vmem_limit = 63 * 1024 * 1024
    block_rows = round_up(rows // devices, 8)
    bits = replicas.bit_length() - 1
    qkv_width = queries.shape[1] + 2 * keys.shape[1]
    qkv_rows = round_up(width // shards, 16) + 16
    out_rows = round_up(out_full.shape[0] // shards, 16)
    members, half_rows = ff_grads.shape[:2]
    low = jnp.bfloat16
    full = jnp.float32
    vmem = pl.BlockSpec(memory_space=pltpu.VMEM)
    hbm = pl.BlockSpec(memory_space=pl.ANY)
    dma = pltpu.SemaphoreType.DMA

    def chain_scratch(count, cols):
        return [
            pltpu.VMEM((2, line, count, cols), low),
            pltpu.VMEM((line, count, cols), low),
            pltpu.VMEM((2, line - 1, count, cols), low),
            pltpu.VMEM((bits + 1, count, cols), low),
            pltpu.VMEM((bits, count, cols), low),
        ]

    return pl.pallas_call(
        functools.partial(back_kernel, line, replicas),
        out_shape=(
            jax.ShapeDtypeStruct((members, half_rows // 4, width), low),
            jax.ShapeDtypeStruct((members, half_rows // 4, width), low),
            jax.ShapeDtypeStruct((qkv_rows, qkv_width), low),
            jax.ShapeDtypeStruct((out_rows, width), low),
            jax.ShapeDtypeStruct((rows, width), full),
            jax.ShapeDtypeStruct((rows, width), full),
        ),
        in_specs=[hbm] * held + [vmem] * (len(small) - held) + [hbm] * 3,
        out_specs=(hbm,) * 4 + (vmem,) * 2,
        scratch_shapes=[
            pltpu.VMEM((width, qkv_width), low),
            pltpu.VMEM(out_full.shape, low),
            pltpu.VMEM(ff_grads.shape, low),
            pltpu.VMEM(ff_grads.shape, low),
            pltpu.VMEM((members - EARLY, 2, half_rows // 4, width), low),
            pltpu.VMEM(
                (members, 2, half_rows // 4 - half_rows // (2 * replicas), width), low
            ),
            *chain_scratch(qkv_rows - 16, queries.shape[1]),
            *chain_scratch(qkv_rows, 2 * keys.shape[1]),
            *chain_scratch(out_rows, width),
            pltpu.VMEM((rows, qkv_width), low),
            pltpu.VMEM((rows, keys.shape[1]), full),
            pltpu.VMEM((rows, keys.shape[1]), full),
            pltpu.VMEM((devices * block_rows, rows), low),
            pltpu.VMEM((2, devices, block_rows, width), low),
            pltpu.VMEM((2, devices, block_rows, width), low),
            [pltpu.VMEM(operand.shape, operand.dtype) for operand in small[:held]],
            dma((held,)),
            dma((3,)),
            dma((3 + 2 * members,)),
            dma((2, members, 2, bits)),
            dma((2, members, 2, bits)),
            dma((3,)),
            dma((3,)),
            dma((3, 2, line - 1)),
            dma((3, 2, line - 1)),
            dma((4, bits)),
            dma((4, bits)),
            dma((2, devices)),
            dma((2, devices)),
        ],
        compiler_params=pltpu.CompilerParams(
            collective_id=1, has_side_effects=True, vmem_limit_bytes=vmem_limit
        ),
        cost_estimate=pl.CostEstimate(
            flops=16 * rows * width * qkv_width,
            bytes_accessed=4 * members * half_rows * width,
            transcendentals=2 * rows * rows * 4,
        ),
    )(*small, first_full, out_full, ff_grads)


def bring_kernel(
    line,
    replicas,
    near_weights,
    tokens_ref,
    cotangent_ref,
    deal_ref,
    gains_in,
    qkv_in,
    out_in,
    lengths_ref,
    frequency_ref,
    gu_hbm,
    down_hbm,
    inputs_ref,
    upstream_ref,
    normed_ref,
    queries_ref,
    keys_ref,
    values_ref,
    attended_ref,
    branch_ref,
    middle_ref,
    normed_two_ref,
    gains_ref,
    cosine_ref,
    sine_ref,
    doc_col_ref,
    doc_row_ref,
    qkv_hbm,
    outw_hbm,
    weights_hbm,
    w_qkv,
    w_out,
    gain_blocks,
    weights,
    tiles,
    sent,
    arrived,
    projected,
    load_sems,
    store_sems,
    row_send,
    row_recv,
    line_send,
    line_recv,
    rep_send,
    rep_recv,
    pair_send,
    pair_recv,
    gain_send,
    gain_recv,
    sibling_send,
    sibling_recv,
):
    rep = lax.axis_index("rep")
    shard = lax.axis_index("shard")
    shards = 2 * line
    devices = replicas * shards
    me = rep * shards + shard
    core = lax.rem(shard, 2)
    place = lax.div(shard, 2)
    sibling = (rep, shard + 1 - 2 * core)
    share = min(4, replicas)
    quarter = lax.rem(rep, share)
    full = jnp.float32
    low = jnp.bfloat16
    rows, width = tokens_ref.shape
    peer_rows = rows // devices
    block_rows = sent.shape[2]
    units = gu_hbm.shape[1]
    half = weights.shape[1] // 2
    tile_rows = tiles.shape[1]
    tile_count = units // tile_rows
    depth = tiles.shape[0]
    key_width = keys_ref.shape[1]
    query_width = queries_ref.shape[1]
    heads = query_width // key_width
    half_key = key_width // 2

    def tile_load(turn):
        member, at = turn // tile_count, turn % tile_count * tile_rows
        source = down_hbm if member == 0 else gu_hbm.at[member - 1]
        return pltpu.make_async_copy(
            source.at[pl.ds(at, tile_rows)], tiles.at[turn % depth], load_sems.at[turn % depth]
        )

    for turn in range(min(depth, 3 * tile_count)):
        tile_load(turn).start()

    barrier = pltpu.get_barrier_semaphore()

    @pl.loop(1, devices)
    def _(hop):
        peer = lax.rem(me + hop, devices)
        pl.semaphore_signal(
            barrier,
            inc=1,
            device_id=(lax.div(peer, shards), lax.rem(peer, shards)),
            device_id_type=MESH,
        )

    if near_weights:
        w_qkv[shard] = qkv_in[...].astype(low)

    down_ids = lax.broadcasted_iota(jnp.int32, (rows, rows), 0)
    along_ids = lax.broadcasted_iota(jnp.int32, (rows, rows), 1)
    eye = down_ids == along_ids

    def to_column(row):
        return jnp.sum(jnp.where(eye, row, 0), axis=1, keepdims=True)

    def to_row(column):
        return jnp.sum(jnp.where(eye, column, 0), axis=0, keepdims=True)

    def spread(places):
        return lax.div(places, peer_rows) * block_rows + lax.rem(places, peer_rows)

    own_deal = deal_row(deal_ref, me, rows)
    send_place = jnp.sum((to_column(own_deal) < own_deal).astype(jnp.int32), axis=0, keepdims=True)
    packed = devices * block_rows
    picker = (
        lax.broadcasted_iota(jnp.int32, (packed, rows), 0) == spread(send_place)
    ).astype(low)

    def pack(kind, source):
        sent[kind] = (
            jnp.dot(picker, source[...], preferred_element_type=full)
            .reshape(devices, block_rows, width)
            .astype(low)
        )
        arrived[kind, me] = sent[kind, me]

    pack(0, tokens_ref)
    pl.semaphore_wait(barrier, devices - 1)

    def row_copy(kind, hop, peer, source):
        return pltpu.make_async_remote_copy(
            src_ref=sent.at[kind, peer],
            dst_ref=arrived.at[kind, source],
            send_sem=row_send.at[kind, hop],
            recv_sem=row_recv.at[kind, hop],
            device_id=(lax.div(peer, shards), lax.rem(peer, shards)),
            device_id_type=MESH,
        )

    def rows_start(kind):
        @pl.loop(1, devices)
        def _(hop):
            row_copy(kind, hop, lax.rem(me + hop, devices), me).start()

    def rows_arrive(kind):
        @pl.loop(1, devices)
        def _(hop):
            source = lax.rem(me + devices - hop, devices)
            row_copy(kind, hop, source, source).wait_recv()

    gathered = (w_qkv, w_out)

    def part_of(kind, member, portion):
        buffer = gathered[kind]
        if kind == 0:
            size = buffer.shape[2] // share
            return buffer.at[member, :, pl.ds(pl.multiple_of(portion * size, LANES), size)]
        size = buffer.shape[1] // share
        return buffer.at[member, pl.ds(pl.multiple_of(portion * size, 16), size)]

    def line_copy(kind, target, source):
        part = part_of(kind, 2 * source + core, quarter)
        return pltpu.make_async_remote_copy(
            src_ref=part,
            dst_ref=part,
            send_sem=line_send.at[kind, target],
            recv_sem=line_recv.at[kind, source],
            device_id=(rep, 2 * target + core),
            device_id_type=MESH,
        )

    def rep_copy(kind, block, hop, portion):
        part = part_of(kind, 2 * block + core, portion)
        return pltpu.make_async_remote_copy(
            src_ref=part,
            dst_ref=part,
            send_sem=rep_send.at[kind, block, hop],
            recv_sem=rep_recv.at[kind, block, portion],
            device_id=(rep - quarter + lax.rem(quarter + hop, share), shard),
            device_id_type=MESH,
        )

    def pair_copy(kind, block, side):
        buffer = gathered[kind]
        return pltpu.make_async_remote_copy(
            src_ref=buffer.at[2 * block + side],
            dst_ref=buffer.at[2 * block + side],
            send_sem=pair_send.at[kind, block],
            recv_sem=pair_recv.at[kind, block],
            device_id=sibling,
            device_id_type=MESH,
        )

    def gain_copy(hop, source):
        return pltpu.make_async_remote_copy(
            src_ref=gain_blocks.at[source],
            dst_ref=gain_blocks.at[source],
            send_sem=gain_send.at[hop],
            recv_sem=gain_recv.at[hop],
            device_id=(rep, lax.rem(shard + hop, shards)),
            device_id_type=MESH,
        )

    def others():
        return [lax.rem(place + hop, line) for hop in range(1, line)]

    def line_start(kind):
        for target in others():
            line_copy(kind, target, place).start()
        pair_copy(kind, place, core).start()

    def line_pass(kind):
        for source in others():
            line_copy(kind, source, source).wait_recv()
            for hop in range(1, share):
                rep_copy(kind, source, hop, quarter).start()

    def rep_pass(kind):
        for block in others():
            for hop in range(1, share):
                rep_copy(kind, block, hop, lax.rem(quarter + hop, share)).wait_recv()
            pair_copy(kind, block, core).start()

    def pair_arrive(kind):
        for block in range(line):
            pair_copy(kind, block, 1 - core).wait_recv()

    if near_weights:
        line_start(0)
    rows_start(0)
    if near_weights:
        w_out[shard] = out_in[...].astype(low)
        line_start(1)
        gain_blocks[shard] = jnp.zeros(gain_blocks.shape[1:], low)
        gain_blocks[shard, : gains_in.shape[0], : gains_in.shape[1]] = gains_in[...].astype(low)
        for hop in range(1, shards):
            gain_copy(hop, shard).start()

    def sibling_copy(member):
        return pltpu.make_async_remote_copy(
            src_ref=weights.at[member, pl.ds(0, half)],
            dst_ref=weights.at[member, pl.ds(half, half)],
            send_sem=sibling_send.at[member],
            recv_sem=sibling_recv.at[member],
            device_id=sibling,
            device_id_type=MESH,
        )

    def cast(begin, end):
        for turn in range(begin, end):
            member, at = turn // tile_count, turn % tile_count * tile_rows
            tile_load(turn).wait()
            weights[member, at : at + tile_rows, :] = tiles[turn % depth].astype(low)
            if turn + depth < 3 * tile_count:
                tile_load(turn + depth).start()

    if half > units:
        for member in range(3):
            weights[member, units:half, :] = jnp.zeros((half - units, width), low)

    own_slots = lax.broadcasted_iota(jnp.int32, (rows, rows), 0) + me * rows

    def find(source, total):
        return total + jnp.where(deal_row(deal_ref, source, rows) == own_slots, source, 0)

    found = lax.fori_loop(0, devices, find, jnp.zeros((rows, rows), jnp.int32))
    source = jnp.sum(found, axis=1, keepdims=True)
    earlier = (to_row(source) == source) & (along_ids < down_ids)
    recv_place = source * peer_rows + jnp.sum(earlier.astype(jnp.int32), axis=1, keepdims=True)
    placer = (
        lax.broadcasted_iota(jnp.int32, (rows, packed), 1) == spread(recv_place)
    ).astype(low)

    ids = lax.broadcasted_iota(jnp.int32, (rows, 1), 0)
    end = jnp.int32(0)
    document = jnp.zeros((rows, 1), jnp.int32)
    begin = jnp.zeros((rows, 1), jnp.int32)
    for member in range(lengths_ref.shape[1]):
        end = end + lengths_ref[0, member]
        passed = ids >= end
        document = document + passed.astype(jnp.int32)
        begin = jnp.where(passed, end, begin)
    doc_col_ref[...] = document
    doc_row_ref[...] = to_row(document)
    angles = (ids - begin).astype(full) * frequency_ref[...]
    cosine_ref[...] = jnp.cos(angles)
    sine_ref[...] = jnp.sin(angles)
    if near_weights:
        line_pass(0)
    pack(1, cotangent_ref)
    for member in range(3):
        cast(member * tile_count, (member + 1) * tile_count)
        sibling_copy(member).start()
    near_stores = [
        pltpu.make_async_copy(
            weights.at[member, pl.ds(0, half)],
            weights_hbm.at[member, pl.ds(0, half)],
            store_sems.at[2 + member],
        )
        for member in range(3)
    ]
    for store in near_stores:
        store.start()

    def placed(kind):
        stacked = arrived[kind].astype(full).reshape(packed, width).astype(low)
        return jnp.dot(placer, stacked, preferred_element_type=full)

    if near_weights:
        for hop in range(1, shards):
            gain_copy(hop, lax.rem(shard + shards - hop, shards)).wait_recv()
        span = gains_in.shape[1]
        line_ids = lax.broadcasted_iota(jnp.int32, (gain_blocks.shape[2], width), 0)
        lane_ids = lax.broadcasted_iota(jnp.int32, (gain_blocks.shape[2], width), 1)
        joined = jnp.zeros((gain_blocks.shape[1], width), full)
        for member in range(shards):
            move = ((lane_ids - member * span == line_ids) & (line_ids < span)).astype(low)
            joined = joined + jnp.dot(gain_blocks[member], move, preferred_element_type=full)
        gains_ref[...] = joined[: gains_ref.shape[0]]
        rep_pass(0)
    else:
        gains_ref[...] = gains_in[...]
    rows_arrive(0)
    inputs = placed(0)
    inputs_ref[...] = inputs.astype(low)
    normed_ref[...] = (inputs * rms_scale(inputs) * gains_ref[0:1, :]).astype(low)
    if near_weights:
        line_pass(1)
    rows_start(1)
    if near_weights:
        pair_arrive(0)
        qkv_matrix = w_qkv[...].reshape(width, w_qkv.shape[2])
    else:
        qkv_matrix = qkv_in[...]
    projected[...] = jnp.dot(normed_ref[...], qkv_matrix, preferred_element_type=full)

    def turned(start):
        front = projected[:, pl.ds(start, half_key)]
        back = projected[:, pl.ds(start + half_key, half_key)]
        cosine, sine = cosine_ref[...], sine_ref[...]
        return (
            (front * cosine - back * sine).astype(low),
            (back * cosine + front * sine).astype(low),
        )

    keys_ref[:, :half_key], keys_ref[:, half_key:] = turned(query_width)
    values_ref[...] = projected[:, query_width + key_width :].astype(low)

    for head in range(heads):
        if near_weights and head == heads // 2:
            rep_pass(1)
        start = head * key_width
        cols = pl.ds(start, key_width)
        front, back = turned(start)
        queries_ref[:, pl.ds(start, half_key)] = front
        queries_ref[:, pl.ds(start + half_key, half_key)] = back
        allowed = (doc_col_ref[...] == doc_row_ref[...]) & (
            lax.broadcasted_iota(jnp.int32, (rows, rows), 0)
            >= lax.broadcasted_iota(jnp.int32, (rows, rows), 1)
        )
        scores = against_cols(queries_ref[:, cols], keys_ref[...]) * (HD ** (-0.5) / CAP_LIMIT)
        capped = jnp.where(allowed, CAP_LIMIT * jnp.tanh(scores), MASKED_SCORE)
        powers = jnp.exp(capped - jnp.max(capped, axis=-1, keepdims=True))
        probs = powers / jnp.sum(powers, axis=-1, keepdims=True)
        attended_ref[:, cols] = jnp.dot(
            probs.astype(low), values_ref[...], preferred_element_type=full
        ).astype(low)

    if near_weights:
        pair_arrive(1)
        out_matrix = w_out[...].reshape(query_width, width)
    else:
        out_matrix = out_in[...]
    stores = []
    if near_weights:
        stores.append(pltpu.make_async_copy(w_qkv, qkv_hbm, store_sems.at[0]))
        stores.append(pltpu.make_async_copy(w_out, outw_hbm, store_sems.at[1]))
    else:
        stores.append(pltpu.make_async_copy(qkv_in, qkv_hbm, store_sems.at[0]))
        stores.append(pltpu.make_async_copy(out_in, outw_hbm, store_sems.at[1]))
    for store in stores:
        store.start()
    for member in range(3):
        sibling_copy(member).wait_recv()
        store = pltpu.make_async_copy(
            weights.at[member, pl.ds(half, half)],
            weights_hbm.at[member, pl.ds(half, half)],
            store_sems.at[5 + member],
        )
        store.start()
        stores.append(store)
    branch = jnp.dot(attended_ref[...], out_matrix, preferred_element_type=full)
    branch_ref[...] = branch
    middle = inputs_ref[...].astype(full) + branch * rms_scale(branch) * gains_ref[1:2, :]
    middle_ref[...] = middle
    normed_two_ref[...] = (middle * rms_scale(middle) * gains_ref[2:3, :]).astype(low)
    rows_arrive(1)
    upstream_ref[...] = placed(1).astype(low)
    stores.extend(near_stores)

    for kind in range(2):

        @pl.loop(1, devices)
        def _(hop, kind=kind):
            row_copy(kind, hop, lax.rem(me + hop, devices), me).wait_send()

        if near_weights:
            for block in others():
                line_copy(kind, block, place).wait_send()
                for hop in range(1, share):
                    rep_copy(kind, block, hop, quarter).wait_send()
            for block in range(line):
                pair_copy(kind, block, core).wait_send()
    if near_weights:
        for hop in range(1, shards):
            gain_copy(hop, shard).wait_send()
    for member in range(3):
        sibling_copy(member).wait_send()
    for store in stores:
        store.wait()


def bring_and_attend(
    line, replicas, near_weights, tokens, cotangent, deal, small, gu, down, key_width
):
    gains_in, qkv_in, out_in = small[:3]
    rows, width = tokens.shape
    shards = 2 * line
    devices = replicas * shards
    share = min(4, replicas)
    block_rows = round_up(rows // devices, 8)
    units = down.shape[0]
    half = round_up(units, LANES)
    low = jnp.bfloat16
    full = jnp.float32
    vmem = pl.BlockSpec(memory_space=pltpu.VMEM)
    hbm = pl.BlockSpec(memory_space=pl.ANY)
    dma = pltpu.SemaphoreType.DMA
    qkv_width = qkv_in.shape[1]
    query_width = qkv_width - 2 * key_width
    if near_weights:
        qkv_shape = (shards, *qkv_in.shape)
        out_shape = (shards, *out_in.shape)
    else:
        qkv_shape = qkv_in.shape
        out_shape = out_in.shape
    tile_rows = max(size for size in range(16, 145, 16) if units % size == 0)
    hold = near_weights
    qkv_scratch = qkv_shape if hold else (shards, 16, LANES)
    out_scratch = out_shape if hold else (shards, 16, LANES)
    gain_lanes = round_up(width // shards, LANES) if hold else LANES

    def array(shape, dtype):
        return jax.ShapeDtypeStruct(shape, dtype)

    return pl.pallas_call(
        functools.partial(bring_kernel, line, replicas, near_weights),
        out_shape=(
            array((rows, width), low),
            array((rows, width), low),
            array((rows, width), low),
            array((rows, query_width), low),
            array((rows, key_width), low),
            array((rows, key_width), low),
            array((rows, query_width), low),
            array((rows, width), full),
            array((rows, width), full),
            array((rows, width), low),
            array((4, width), full),
            array((rows, key_width // 2), full),
            array((rows, key_width // 2), full),
            array((rows, 1), jnp.int32),
            array((1, rows), jnp.int32),
            array(qkv_shape, low),
            array(out_shape, low),
            array((3, 2 * half, width), low),
        ),
        in_specs=[vmem] * 6
        + [pl.BlockSpec(memory_space=pltpu.SMEM), vmem]
        + [hbm] * 2,
        out_specs=(vmem,) * 15 + (hbm,) * 3,
        scratch_shapes=[
            pltpu.VMEM(qkv_scratch, low),
            pltpu.VMEM(out_scratch, low),
            pltpu.VMEM((shards, 16, gain_lanes), low),
            pltpu.VMEM((3, 2 * half, width), low),
            pltpu.VMEM((4, tile_rows, width), full),
            pltpu.VMEM((2, devices, block_rows, width), low),
            pltpu.VMEM((2, devices, block_rows, width), low),
            pltpu.VMEM((rows, qkv_width), full),
            dma((4,)),
            dma((8,)),
            dma((2, devices)),
            dma((2, devices)),
            dma((2, line)),
            dma((2, line)),
            dma((2, line, share)),
            dma((2, line, share)),
            dma((2, line)),
            dma((2, line)),
            dma((shards,)),
            dma((shards,)),
            dma((3,)),
            dma((3,)),
        ],
        compiler_params=pltpu.CompilerParams(
            collective_id=2, has_side_effects=True, vmem_limit_bytes=63 * 1024 * 1024
        ),
        cost_estimate=pl.CostEstimate(
            flops=6 * rows * width * qkv_width,
            bytes_accessed=3 * units * width * 8,
            transcendentals=2 * rows * rows * 4,
        ),
    )(tokens, cotangent, deal, *small, gu, down)


def adam_half_kernel(which, first_half, second_half, *refs):
    del which
    inputs, results = refs[:6], refs[-10:]
    part, member = pl.program_id(0), pl.program_id(1)
    gradient = jnp.where(part == 0, first_half[0], second_half[0]).astype(jnp.float32)

    def step(rows_in, rows_out, rate, decay):
        master, first, second = (ref[...].reshape(gradient.shape) for ref in rows_in)
        updated, moment, square = adam_values(master, gradient, first, second, rate, decay)
        for ref, value in zip(rows_out, (updated, moment, square, gradient, updated)):
            ref[...] = value.astype(ref.dtype).reshape(ref.shape)

    @pl.when(member == 0)
    def _():
        step(inputs[:3], results[:5], LEARN_RATES[3], DECAY_RATES[3])

    @pl.when(member > 0)
    def _():
        step(inputs[3:], results[5:], LEARN_RATES[2], DECAY_RATES[2])


def adam_values(master, gradient, first, second, rate, decay):
    moment = BETA_FIRST * first + (1.0 - BETA_FIRST) * gradient
    square = BETA_SECOND * second + (1.0 - BETA_SECOND) * gradient * gradient
    moment_hat = moment * (1.0 / (1.0 - BETA_FIRST**STEP))
    square_hat = square * (1.0 / (1.0 - BETA_SECOND**STEP))
    updated = master - rate * (moment_hat / (jnp.sqrt(square_hat) + ADAM_EPS) + decay * master)
    return updated, moment, square


def adam_stream_kernel(begun, which, first_half, second_half, *refs):
    sources, refs = refs[:6], refs[6 + begun :]
    results, (taken, grads, given, copies, in_sems, out_sems) = refs[:10], refs[10:]
    depth, tile = taken.shape[0], taken.shape[2]
    units = sources[0].shape[0]
    members = first_half.shape[0]
    order = [
        (part, sub, member) for part in range(2) for sub in range(2) for member in range(members)
    ]

    def rows_of(part, sub):
        begin = (part * 4 + which[part] * 2) * tile
        start = begin + sub * tile
        if part == 1 and sub == 1:
            start = jnp.minimum(start, units - tile)
        return at_rows(start, tile), at_rows(start - begin, tile)

    def view(ref, member, span):
        return ref.at[span] if member == 0 else ref.at[member - 1, span]

    def loads(turn):
        part, sub, member = order[turn]
        span, grad_span = rows_of(part, sub)
        slot = turn % depth
        group = sources[:3] if member == 0 else sources[3:]
        pairs = [(view(ref, member, span), taken.at[slot, at]) for at, ref in enumerate(group)]
        half = (first_half, second_half)[part]
        pairs.append((half.at[member, grad_span], grads.at[slot]))
        return [
            pltpu.make_async_copy(source, target, in_sems.at[slot, at])
            for at, (source, target) in enumerate(pairs)
        ]

    def stores(turn):
        part, sub, member = order[turn]
        span, _ = rows_of(part, sub)
        slot = turn % 2
        group = results[:5] if member == 0 else results[5:]
        held = [given.at[slot, at] for at in range(4)] + [copies.at[slot]]
        return [
            pltpu.make_async_copy(source, view(ref, member, span), out_sems.at[slot, at])
            for at, (source, ref) in enumerate(zip(held, group))
        ]

    for turn in range(depth):
        for load in loads(turn):
            load.start()
    for turn, (_, _, member) in enumerate(order):
        slot, out = turn % depth, turn % 2
        rate, decay = (LEARN_RATES[3], DECAY_RATES[3]) if member == 0 else (
            LEARN_RATES[2],
            DECAY_RATES[2],
        )
        for load in loads(turn):
            load.wait()
        if turn >= 2:
            for store in stores(turn - 2):
                store.wait()

        @pl.loop(0, tile // 16)
        def _(group, slot=slot, out=out, rate=rate, decay=decay):
            span = at_rows(group * 16, 16)
            gradient = grads[slot, span, :].astype(jnp.float32)
            updated, moment, square = adam_values(
                taken[slot, 0, span, :],
                gradient,
                taken[slot, 1, span, :],
                taken[slot, 2, span, :],
                rate,
                decay,
            )
            for at, value in enumerate((updated, moment, square, gradient)):
                given[out, at, span, :] = value
            copies[out, span, :] = updated.astype(copies.dtype)

        for store in stores(turn):
            store.start()
        if turn + depth < len(order):
            for load in loads(turn + depth):
                load.start()
    for turn in range(len(order) - 2, len(order)):
        for store in stores(turn):
            store.wait()


def adam_stream(which, halves, arrays, begun=()):
    members, half_rows, width = halves[0].shape
    tile = half_rows // 2
    hbm = pl.BlockSpec(memory_space=pl.ANY)
    full, low = jnp.float32, jnp.bfloat16
    shapes = []
    for like in (arrays[0], arrays[3]):
        shapes.extend([jax.ShapeDtypeStruct(like.shape, full)] * 4)
        shapes.append(jax.ShapeDtypeStruct(like.shape, low))
    count = members * half_rows * width * 2
    return pl.pallas_call(
        functools.partial(adam_stream_kernel, len(begun)),
        out_shape=tuple(shapes),
        in_specs=[pl.BlockSpec(memory_space=pltpu.SMEM)] + [hbm] * (8 + len(begun)),
        out_specs=(hbm,) * 10,
        scratch_shapes=[
            pltpu.VMEM((3, 3, tile, width), full),
            pltpu.VMEM((3, tile, width), low),
            pltpu.VMEM((2, 4, tile, width), full),
            pltpu.VMEM((2, tile, width), low),
            pltpu.SemaphoreType.DMA((3, 4)),
            pltpu.SemaphoreType.DMA((2, 5)),
        ],
        input_output_aliases={9 + at: at for at in range(len(begun))},
        compiler_params=pltpu.CompilerParams(vmem_limit_bytes=60 * 1024 * 1024),
        cost_estimate=pl.CostEstimate(
            flops=16 * count, bytes_accessed=32 * count, transcendentals=2 * count
        ),
    )(which, *halves, *arrays, *begun)


def adam_half(which, halves, arrays, begun=()):
    members, half_rows, width = halves[0].shape
    tile = half_rows // 2
    down, gu = arrays[0], arrays[3]
    if down.shape[0] - 3 * half_rows >= tile:
        return adam_stream(which, halves, arrays, begun)

    def down_at(part, member, sub, chosen):
        return (part * 4 + chosen[part] * 2 + jnp.where(member == 0, sub, 1), 0)

    def gu_at(part, member, sub, chosen):
        row = part * 4 + chosen[part] * 2 + jnp.where(member == 0, 0, sub)
        return (jnp.maximum(member - 1, 0), row, 0)

    def first_at(part, member, sub, chosen):
        return (jnp.where(part == 0, member, members - 1), jnp.where(part == 0, sub, 1), 0)

    def second_at(part, member, sub, chosen):
        return (jnp.where(part == 0, 0, member), jnp.where(part == 0, 0, sub), 0)

    down_block = pl.BlockSpec((tile, width), down_at)
    gu_block = pl.BlockSpec((1, tile, width), gu_at)
    half_block = (1, tile, width)
    hbm = pl.BlockSpec(memory_space=pl.ANY)
    shapes = []
    for like in (down, gu):
        shapes.extend([jax.ShapeDtypeStruct(like.shape, jnp.float32)] * 4)
        shapes.append(jax.ShapeDtypeStruct(like.shape, jnp.bfloat16))
    count = members * half_rows * width * 2
    return pl.pallas_call(
        adam_half_kernel,
        out_shape=tuple(shapes),
        grid_spec=pltpu.PrefetchScalarGridSpec(
            num_scalar_prefetch=1,
            grid=(2, members, 2),
            in_specs=[
                pl.BlockSpec(half_block, first_at),
                pl.BlockSpec(half_block, second_at),
                *[down_block] * 3,
                *[gu_block] * 3,
                *[hbm] * len(begun),
            ],
            out_specs=(*[down_block] * 5, *[gu_block] * 5),
        ),
        input_output_aliases={9 + at: at for at in range(len(begun))},
        compiler_params=pltpu.CompilerParams(vmem_limit_bytes=60 * 1024 * 1024),
        cost_estimate=pl.CostEstimate(
            flops=16 * count, bytes_accessed=32 * count, transcendentals=2 * count
        ),
    )(which, *halves, *arrays, *begun)


def local(
    tokens,
    cotangent,
    lengths,
    deal,
    w_qkv,
    w_out,
    w_gu,
    w_down,
    gains,
    first_qkv,
    first_out,
    first_gu,
    first_down,
    first_gains,
    second_qkv,
    second_out,
    second_gu,
    second_down,
    second_gains,
):
    row_count, width = tokens.shape
    shards = lax.axis_size("shard")
    replicas = lax.axis_size("rep")
    line = shards // 2
    devices = replicas * shards
    deal_blocks = deal.reshape(deal.shape[0] // LANES, LANES)
    exponent = np.arange(HD // 2, dtype=np.float32) * np.float32(-2.0 / HD)
    frequency = jnp.asarray((np.float32(ROPE_BASE) ** exponent)[None, :])
    near_weights = w_qkv.shape[0] % 16 == 0
    if near_weights:
        first_weights = (gains, w_qkv, w_out)
    else:
        first_weights = (
            lax.all_gather(gains.astype(jnp.bfloat16), "shard", axis=1, tiled=True).astype(
                jnp.float32
            ),
            lax.all_gather(w_qkv.astype(jnp.bfloat16), "shard", axis=0, tiled=True),
            lax.all_gather(w_out.astype(jnp.bfloat16), "shard", axis=0, tiled=True),
        )
    (
        inputs,
        upstream,
        normed_one,
        queries,
        key_rows,
        value_rows,
        attended,
        branch,
        middle,
        normed_two,
        gain_values,
        cosine_table,
        sine_table,
        doc_col,
        doc_row,
        full_qkv,
        full_out,
        ff_weights,
    ) = bring_and_attend(
        line,
        replicas,
        near_weights,
        tokens,
        cotangent,
        deal_blocks,
        (*first_weights, lengths, frequency),
        w_gu,
        w_down,
        HD,
    )
    full_qkv = full_qkv.reshape(width, w_qkv.shape[1])
    full_out = full_out.reshape(H * HD, width)
    output_rows, last_gain_grad, grad_normed_two, ff_grads = feed_forward(
        line,
        replicas,
        normed_two,
        middle,
        upstream,
        gain_values,
        ff_weights,
    )
    first_half, second_half, qkv_sums, out_sums, output, input_grad = back_and_reduce(
        line,
        replicas,
        (
            grad_normed_two,
            middle,
            upstream,
            branch,
            inputs,
            normed_one,
            attended,
            queries,
            key_rows,
            value_rows,
            cosine_table,
            sine_table,
            doc_col,
            doc_row,
            gain_values,
            last_gain_grad,
            output_rows,
            deal_blocks,
        ),
        full_qkv,
        full_out,
        ff_grads,
    )
    output = output.astype(jnp.bfloat16)
    input_grad = input_grad.astype(jnp.bfloat16)

    bits = replicas.bit_length() - 1
    flips = (1, 1 << (bits - 1))
    other_halves = tuple(
        lax.ppermute(half, "rep", [(member, member ^ flip) for member in range(replicas)])
        for half, flip in zip((first_half, second_half), flips)
    )
    rep = lax.axis_index("rep")
    held = jnp.stack([lax.rem(lax.div(rep, flip), 2) for flip in flips]).astype(jnp.int32)
    ff_arrays = (w_down, first_down, second_down, w_gu, first_gu, second_gu)
    begun = adam_half(held, (first_half, second_half), ff_arrays)
    (
        new_down,
        moment_down,
        square_down,
        summed_down,
        copy_down,
        new_gu,
        moment_gu,
        square_gu,
        summed_gu,
        copy_gu,
    ) = adam_half(1 - held, other_halves, ff_arrays, begun)
    summed_qkv = qkv_sums[: w_qkv.shape[0]].astype(jnp.float32)
    summed_out = out_sums[: w_out.shape[0]].astype(jnp.float32)
    gain_span = gains.shape[1]
    gain_rows = qkv_sums[-16:-4, H * HD : H * HD + width // 3]
    summed_gains = lax.dynamic_slice(
        gain_rows.reshape(3, gains.shape[0], width // 3)
        .transpose(1, 0, 2)
        .reshape(gains.shape[0], width),
        (0, lax.axis_index("shard") * gain_span),
        (gains.shape[0], gain_span),
    ).astype(jnp.float32)
    new_qkv, moment_qkv, square_qkv = adamw_step(
        w_qkv, summed_qkv, first_qkv, second_qkv, LEARN_RATES[0], DECAY_RATES[0]
    )
    new_out, moment_out, square_out = adamw_step(
        w_out, summed_out, first_out, second_out, LEARN_RATES[1], DECAY_RATES[1]
    )
    new_gains, moment_gains, square_gains = adamw_step(
        gains, summed_gains, first_gains, second_gains, LEARN_RATES[4], DECAY_RATES[4]
    )
    return (
        output,
        input_grad,
        new_qkv,
        new_out,
        new_gu,
        new_down,
        new_gains,
        moment_qkv,
        moment_out,
        moment_gu,
        moment_down,
        moment_gains,
        square_qkv,
        square_out,
        square_gu,
        square_down,
        square_gains,
        summed_qkv,
        summed_out,
        summed_gu,
        summed_down,
        summed_gains,
        new_qkv.astype(jnp.bfloat16),
        new_out.astype(jnp.bfloat16),
        copy_gu,
        copy_down,
        new_gains.astype(jnp.bfloat16),
    )


def solution(mesh):
    placed = (
        P(("rep", "shard"), None),
        P(("rep", "shard"), None),
        P(("rep", "shard"), None),
        P(),
        P("shard", None),
        P("shard", None),
        P(None, "shard", None),
        P("shard", None),
        P(None, "shard"),
        P("shard", None),
        P("shard", None),
        P(None, "shard", None),
        P("shard", None),
        P(None, "shard"),
        P("shard", None),
        P("shard", None),
        P(None, "shard", None),
        P("shard", None),
        P(None, "shard"),
    )
    return jax.shard_map(
        local,
        mesh=mesh,
        in_specs=placed,
        out_specs=(
            P(("rep", "shard"), None),
            P(("rep", "shard"), None),
            P("shard", None),
            P("shard", None),
            P(None, "shard", None),
            P("shard", None),
            P(None, "shard"),
            P("shard", None),
            P("shard", None),
            P(None, "shard", None),
            P("shard", None),
            P(None, "shard"),
            P("shard", None),
            P("shard", None),
            P(None, "shard", None),
            P("shard", None),
            P(None, "shard"),
            P("shard", None),
            P("shard", None),
            P(None, "shard", None),
            P("shard", None),
            P(None, "shard"),
            P("shard", None),
            P("shard", None),
            P(None, "shard", None),
            P("shard", None),
            P(None, "shard"),
        ),
        check_vma=False,
    )
```

profile of v0, /device:TPU:8, one launch (start us, length us, event | category | flops | bytes accessed | tf_op | source)
XLA Modules:
  0.0 375.5 jit_solution(16833101835269025794)
XLA Ops:
  0.7 67.2 %shard_map.403 = (bf16[256,1152]{1,0:T(8,128)(2,1)}, bf16[256,1152]{1,0:T(8,128)(2,1)}, bf16[256,1152]{1,0:T(8,128)(2,1)}, bf16[256,1024]{1,0:T(8,128)(2,1)}, bf...) custom-call(bf16[256,1152]{1,0:T(8,128)(2,1)} %tokens_ref.1, ...), custom_call_target="tpu_custom_call" | custom-call | flops 2717908992 | bytes 23887872 | tf_op jit(solution)/shard_map/pallas_call | solution.py:1739
  67.9 147.4 %shard_map.404 = (bf16[256,1152]{1,0:T(8,128)(2,1)}, f32[1,1152]{1,0:T(1,128)}, f32[256,1152]{1,0:T(8,128)}, bf16[3,896,1152]{2,1,0:T(8,128)(2,1)}) custom-call(bf16[256,1152]{1,0:T(8,128)(2,1)} %get-tuple-element.75.own_rows, f32[256,1152]{1,0:T(8,128)} %get-tuple-element.76.middle_ref.middle_hbm, ...), custom_call_target="tpu_custom_call" | custom-call | flops 38050725888 | bytes 18579456 | tf_op jit(solution)/shard_map/pallas_call | solution.py:522
  215.3 107.4 %shard_map.405 = (bf16[3,224,1152]{2,1,0:T(8,128)(2,1)}, bf16[3,224,1152]{2,1,0:T(8,128)(2,1)}, bf16[160,1536]{1,0:T(8,128)(2,1)}, bf16[128,1152]{1,0:T(8,128)(2...) custom-call(f32[256,1152]{1,0:T(8,128)} %get-tuple-element.80.back_hbm, ...), custom_call_target="tpu_custom_call" | custom-call | flops 7247757312 | bytes 12386304 | tf_op jit(solution)/shard_map/pallas_call | solution.py:1221
  322.7 0.8 collective-permute-start
  323.4 1.0 collective-permute-start.1
  324.4 2.1 convert_element_type.24
  326.6 2.1 convert_element_type.25
  328.7 0.7 slice.7
  329.5 0.6 broadcast_subtract_fusion
  330.0 0.0 copy-start.8
  330.0 0.0 copy-start.9
  330.1 0.0 copy-start.10
  330.1 0.0 copy-start.1
  330.1 0.0 copy-start.7
  330.1 18.7 %shard_map.406 = (f32[864,1152]{1,0:T(8,128)}, f32[864,1152]{1,0:T(8,128)}, f32[864,1152]{1,0:T(8,128)}, f32[864,1152]{1,0:T(8,128)}, bf16[864,1152]{1,0:T(8,128...) custom-call(s32[2]{0:T(128)} %get-tuple-element.139.which, ...), custom_call_target="tpu_custom_call" | custom-call | flops 24772608 | bytes 49545216 | tf_op jit(solution)/shard_map/pallas_call | solution.py:1925
  348.8 0.0 copy-start
  348.8 0.0 copy-start.4
  348.8 0.0 copy-start.5
  348.8 0.0 copy-start.6
  348.8 0.0 copy-done.8
  348.8 0.0 copy-done.9
  348.8 0.0 copy-done.10
  348.8 0.7 fusion.3
  349.5 0.0 copy-done.1
  349.5 0.0 copy-done.7
  349.5 3.0 fusion.5
  352.6 0.0 copy-done
  352.6 0.0 copy-done.4
  352.6 0.0 copy-done.5
  352.6 0.0 copy-done.6
  352.6 2.2 fusion.7
  354.8 0.0 collective-permute-done.first_half
  354.8 0.0 copy-start.2
  354.8 0.0 collective-permute-done.1.second_half
  354.8 0.0 copy-start.3
  354.8 1.1 copy-done.2
  356.0 0.5 copy-done.3
  356.5 18.5 %shard_map.407 = (f32[864,1152]{1,0:T(8,128)}, f32[864,1152]{1,0:T(8,128)}, f32[864,1152]{1,0:T(8,128)}, f32[864,1152]{1,0:T(8,128)}, bf16[864,1152]{1,0:T(8,128...) custom-call(s32[2]{0:T(128)} %get-tuple-element.138.which, ...), custom_call_target="tpu_custom_call", output_to_operand_aliasing={{0}: (9, {}), {1}: (10, {}), {2}: (11, {}), {3}: (12, {}), ... | custom-call | flops 24772608 | bytes 49545216 | tf_op jit(solution)/shard_map/pallas_call | solution.py:1925
  (1 shorter events, 0.0 us)
Async XLA Ops:
  322.7 32.2 %collective-permute-start = (bf16[3,224,1152]{2,1,0:T(8,128)(2,1)}, bf16[3,224,1152]{2,1,0:T(8,128)(2,1)S(1)}, u32[]{:S(2)}, u32[]{:S(2)}) collective-permute-start(bf16[3,224,1152]{2,1,0:T(8,128)(2,1)} %get-tuple-element.101.first_half), channel_id=1, source_target_pairs={{0,8},{8,0},{16,24},{24,16},{1,9},{9,1},{17,25},{25,17},{2,10},{10... | collective-permute-start | bytes 4644872 | tf_op jit(solution)/shard_map/ppermute | solution.py:2113
  323.4 31.4 %collective-permute-start.1 = (bf16[3,224,1152]{2,1,0:T(8,128)(2,1)}, bf16[3,224,1152]{2,1,0:T(8,128)(2,1)S(1)}, u32[]{:S(2)}, u32[]{:S(2)}) collective-permute-start(bf16[3,224,1152]{2,1,0:T(8,128)(2,1)} %get-tuple-element.102.second_half), channel_id=1, source_target_pairs={{0,16},{8,24},{16,0},{24,8},{1,17},{9,25},{17,1},{25,9},{2,18},{10... | collective-permute-start | bytes 4644872 | tf_op jit(solution)/shard_map/ppermute | solution.py:2113
  330.0 18.8 %copy-start.8 = (f32[4,144]{1,0:T(4,128)S(1)}, f32[4,144]{1,0:T(4,128)}, u32[]{:S(2)}) copy-start(f32[4,144]{1,0:T(4,128)} %gains_in.1) | copy-start | bytes 6916
  330.0 18.8 %copy-start.9 = (f32[4,144]{1,0:T(4,128)S(1)}, f32[4,144]{1,0:T(4,128)}, u32[]{:S(2)}) copy-start(f32[4,144]{1,0:T(4,128)} %param.33) | copy-start | bytes 6916
  330.1 18.8 %copy-start.10 = (f32[4,144]{1,0:T(4,128)S(1)}, f32[4,144]{1,0:T(4,128)}, u32[]{:S(2)}) copy-start(f32[4,144]{1,0:T(4,128)} %param.38) | copy-start | bytes 6916
  330.1 19.5 %copy-start.1 = (f32[128,1152]{1,0:T(8,128)S(1)}, f32[128,1152]{1,0:T(8,128)}, u32[]{:S(2)}) copy-start(f32[128,1152]{1,0:T(8,128)} %out_in.1) | copy-start | bytes 1769476
  330.1 19.5 %copy-start.7 = (bf16[128,1152]{1,0:T(8,128)(2,1)S(1)}, bf16[128,1152]{1,0:T(8,128)(2,1)}, u32[]{:S(2)}) copy-start(bf16[128,1152]{1,0:T(8,128)(2,1)} %get-tuple-element.100) | copy-start | bytes 884740
  348.8 3.8 %copy-start = (f32[144,1536]{1,0:T(8,128)S(1)}, f32[144,1536]{1,0:T(8,128)}, u32[]{:S(2)}) copy-start(f32[144,1536]{1,0:T(8,128)} %qkv_in.1) | copy-start | bytes 2654212
  348.8 3.8 %copy-start.4 = (f32[144,1536]{1,0:T(8,128)S(1)}, f32[144,1536]{1,0:T(8,128)}, u32[]{:S(2)}) copy-start(f32[144,1536]{1,0:T(8,128)} %param.29) | copy-start | bytes 2654212
  348.8 3.8 %copy-start.5 = (f32[144,1536]{1,0:T(8,128)S(1)}, f32[144,1536]{1,0:T(8,128)}, u32[]{:S(2)}) copy-start(f32[144,1536]{1,0:T(8,128)} %param.34) | copy-start | bytes 2654212
  348.8 3.8 %copy-start.6 = (bf16[160,1536]{1,0:T(8,128)(2,1)S(1)}, bf16[160,1536]{1,0:T(8,128)(2,1)}, u32[]{:S(2)}) copy-start(bf16[160,1536]{1,0:T(8,128)(2,1)} %get-tuple-element.99) | copy-start | bytes 1474564
  354.8 1.1 copy-start.2
  354.8 1.6 copy-start.3
where the time goes:
time: 383 us; the launch traced here: 375 us
  Pallas kernels  359 us (94%)
  other arithmetic  10.8 us (3%)
    pallas_call x1, Pallas kernels, feed_forward(): pl.pallas_call(functools.partial(feed_kernel, line, replicas), out_shape=...  147 us
    pallas_call x1, Pallas kernels, back_and_reduce(): pl.pallas_call(functools.partial(back_kernel, line, replicas), out_shape=...  107 us
    pallas_call x1, Pallas kernels, bring_and_attend(): pl.pallas_call(functools.partial(bring_kernel, line, replicas, near_weigh...  67.2 us
    pallas_call x2, Pallas kernels, adam_stream(): pl.pallas_call(functools.partial(adam_stream_kernel, len(begun)), out_sha...  37.2 us
  transfers between devices with their start and end apart: 2, of which 0 were waited for; matrix products, arithmetic and copies ran while one was open for 3% of the time, Pallas kernels for 5%

commit v1 on v0

--- a/solution.py
+++ b/solution.py
@@ -455,13 +455,13 @@
     def last_grads(turn):
         @pl.loop(*share(turn, 6, line - 1))
         def _(unit):
-            @pl.when(unit < 3)
+            @pl.when((unit < 2) | (unit == 3))
             def _():
-                far_grad(1, unit)
-
-            @pl.when(unit >= 3)
+                far_grad(1, jnp.minimum(unit, 2))
+
+            @pl.when((unit == 2) | (unit > 3))
             def _():
-                near_grad(unit - 3)
+                near_grad(jnp.where(unit == 2, 0, unit - 3))
 
     def turn_around(part):
         chain_finish(0, part)
@@ -1225,8 +1225,8 @@
             jax.ShapeDtypeStruct((members, half_rows // 4, width), low),
             jax.ShapeDtypeStruct((qkv_rows, qkv_width), low),
             jax.ShapeDtypeStruct((out_rows, width), low),
-            jax.ShapeDtypeStruct((rows, width), full),
-            jax.ShapeDtypeStruct((rows, width), full),
+            jax.ShapeDtypeStruct((rows, width), low),
+            jax.ShapeDtypeStruct((rows, width), low),
         ),
         in_specs=[hbm] * held + [vmem] * (len(small) - held) + [hbm] * 3,
         out_specs=(hbm,) * 4 + (vmem,) * 2,
@@ -1827,9 +1827,12 @@
     return updated, moment, square
 
 
-def adam_stream_kernel(begun, which, first_half, second_half, *refs):
+def adam_stream_kernel(begun, carry, which, first_half, second_half, *refs):
     sources, refs = refs[:6], refs[6 + begun :]
-    results, (taken, grads, given, copies, in_sems, out_sems) = refs[:10], refs[10:]
+    rows_in, refs = refs[:carry], refs[carry:]
+    results, refs = refs[:10], refs[10:]
+    rows_out, refs = refs[:carry], refs[carry:]
+    taken, grads, given, copies, in_sems, out_sems, *passing = refs
     depth, tile = taken.shape[0], taken.shape[2]
     units = sources[0].shape[0]
     members = first_half.shape[0]
@@ -1871,8 +1874,20 @@
             for at, (source, ref) in enumerate(zip(held, group))
         ]
 
+    def passes(outward):
+        held, sems = passing
+        return [
+            pltpu.make_async_copy(held.at[at], rows_out[at], sems.at[1, at])
+            if outward
+            else pltpu.make_async_copy(rows_in[at], held.at[at], sems.at[0, at])
+            for at in range(carry)
+        ]
+
     for turn in range(depth):
         for load in loads(turn):
+            load.start()
+    if carry:
+        for load in passes(False):
             load.start()
     for turn, (_, _, member) in enumerate(order):
         slot, out = turn % depth, turn % 2
@@ -1907,12 +1922,20 @@
         if turn + depth < len(order):
             for load in loads(turn + depth):
                 load.start()
+        if carry and turn == depth:
+            for load in passes(False):
+                load.wait()
+            for store in passes(True):
+                store.start()
     for turn in range(len(order) - 2, len(order)):
         for store in stores(turn):
             store.wait()
-
-
-def adam_stream(which, halves, arrays, begun=()):
+    if carry:
+        for store in passes(True):
+            store.wait()
+
+
+def adam_stream(which, halves, arrays, begun=(), carry=()):
     members, half_rows, width = halves[0].shape
     tile = half_rows // 2
     hbm = pl.BlockSpec(memory_space=pl.ANY)
@@ -1921,12 +1944,16 @@
     for like in (arrays[0], arrays[3]):
         shapes.extend([jax.ShapeDtypeStruct(like.shape, full)] * 4)
         shapes.append(jax.ShapeDtypeStruct(like.shape, low))
+    passing = []
+    if carry:
+        passing.append(pltpu.VMEM((len(carry), *carry[0].shape), carry[0].dtype))
+        passing.append(pltpu.SemaphoreType.DMA((2, len(carry))))
     count = members * half_rows * width * 2
     return pl.pallas_call(
-        functools.partial(adam_stream_kernel, len(begun)),
-        out_shape=tuple(shapes),
-        in_specs=[pl.BlockSpec(memory_space=pltpu.SMEM)] + [hbm] * (8 + len(begun)),
-        out_specs=(hbm,) * 10,
+        functools.partial(adam_stream_kernel, len(begun), len(carry)),
+        out_shape=(*shapes, *(jax.ShapeDtypeStruct(rows.shape, rows.dtype) for rows in carry)),
+        in_specs=[pl.BlockSpec(memory_space=pltpu.SMEM)] + [hbm] * (8 + len((*begun, *carry))),
+        out_specs=(hbm,) * (10 + len(carry)),
         scratch_shapes=[
             pltpu.VMEM((3, 3, tile, width), full),
             pltpu.VMEM((3, tile, width), low),
@@ -1934,21 +1961,22 @@
             pltpu.VMEM((2, tile, width), low),
             pltpu.SemaphoreType.DMA((3, 4)),
             pltpu.SemaphoreType.DMA((2, 5)),
+            *passing,
         ],
         input_output_aliases={9 + at: at for at in range(len(begun))},
         compiler_params=pltpu.CompilerParams(vmem_limit_bytes=60 * 1024 * 1024),
         cost_estimate=pl.CostEstimate(
             flops=16 * count, bytes_accessed=32 * count, transcendentals=2 * count
         ),
-    )(which, *halves, *arrays, *begun)
-
-
-def adam_half(which, halves, arrays, begun=()):
+    )(which, *halves, *arrays, *begun, *carry)
+
+
+def adam_half(which, halves, arrays, begun=(), carry=()):
     members, half_rows, width = halves[0].shape
     tile = half_rows // 2
     down, gu = arrays[0], arrays[3]
     if down.shape[0] - 3 * half_rows >= tile:
-        return adam_stream(which, halves, arrays, begun)
+        return adam_stream(which, halves, arrays, begun, carry)
 
     def down_at(part, member, sub, chosen):
         return (part * 4 + chosen[part] * 2 + jnp.where(member == 0, sub, 1), 0)
@@ -1972,7 +2000,7 @@
         shapes.extend([jax.ShapeDtypeStruct(like.shape, jnp.float32)] * 4)
         shapes.append(jax.ShapeDtypeStruct(like.shape, jnp.bfloat16))
     count = members * half_rows * width * 2
-    return pl.pallas_call(
+    done = pl.pallas_call(
         adam_half_kernel,
         out_shape=tuple(shapes),
         grid_spec=pltpu.PrefetchScalarGridSpec(
@@ -1993,6 +2021,7 @@
             flops=16 * count, bytes_accessed=32 * count, transcendentals=2 * count
         ),
     )(which, *halves, *arrays, *begun)
+    return (*done, *carry)
 
 
 def local(
@@ -2104,9 +2133,6 @@
         full_out,
         ff_grads,
     )
-    output = output.astype(jnp.bfloat16)
-    input_grad = input_grad.astype(jnp.bfloat16)
-
     bits = replicas.bit_length() - 1
     flips = (1, 1 << (bits - 1))
     other_halves = tuple(
@@ -2116,7 +2142,9 @@
     rep = lax.axis_index("rep")
     held = jnp.stack([lax.rem(lax.div(rep, flip), 2) for flip in flips]).astype(jnp.int32)
     ff_arrays = (w_down, first_down, second_down, w_gu, first_gu, second_gu)
-    begun = adam_half(held, (first_half, second_half), ff_arrays)
+    *begun, output, input_grad = adam_half(
+        held, (first_half, second_half), ff_arrays, carry=(output, input_grad)
+    )
     (
         new_down,
         moment_down,

time: 383 us -> 379 us (0.990)
  other arithmetic: 10.8 us -> 6.58 us
    convert_element_type x2 -> x0, other arithmetic: 4.29 us -> none  [the longest x1 2.15 us: local(): input_grad = input_grad.astype(jnp.bfloat16)]
  transfers between devices with their start and end apart: 2 -> 2, of which waited for: 0 -> 2; matrix products, arithmetic and copies ran while one was open for 3% -> 2% of each run, Pallas kernels for 5% -> 5%
where the time goes in v1:
time: 379 us; the launch traced here: 372 us
  Pallas kernels  358 us (94%)
  other arithmetic  6.58 us (2%)
    pallas_call x1, Pallas kernels, feed_forward(): pl.pallas_call(functools.partial(feed_kernel, line, replicas), out_shape=...  147 us
    pallas_call x1, Pallas kernels, back_and_reduce(): pl.pallas_call(functools.partial(back_kernel, line, replicas), out_shape=...  105 us
    pallas_call x1, Pallas kernels, bring_and_attend(): pl.pallas_call(functools.partial(bring_kernel, line, replicas, near_weigh...  67.2 us
    pallas_call x2, Pallas kernels, adam_stream(): pl.pallas_call(functools.partial(adam_stream_kernel, len(begun), len(carr...  37.9 us
  transfers between devices with their start and end apart: 2, of which 2 were waited for; matrix products, arithmetic and copies ran while one was open for 2% of the time, Pallas kernels for 5%

profile of v1, /device:TPU:8, one launch (start us, length us, event | category | flops | bytes accessed | tf_op | source)
XLA Modules:
  0.0 371.8 jit_solution(18436197054734965592)
XLA Ops:
  0.7 67.2 %shard_map.403 = (bf16[256,1152]{1,0:T(8,128)(2,1)}, bf16[256,1152]{1,0:T(8,128)(2,1)}, bf16[256,1152]{1,0:T(8,128)(2,1)}, bf16[256,1024]{1,0:T(8,128)(2,1)}, bf...) custom-call(bf16[256,1152]{1,0:T(8,128)(2,1)} %tokens_ref.1, ...), custom_call_target="tpu_custom_call" | custom-call | flops 2717908992 | bytes 23887872 | tf_op jit(solution)/shard_map/pallas_call | solution.py:1739
  67.9 147.1 %shard_map.404 = (bf16[256,1152]{1,0:T(8,128)(2,1)}, f32[1,1152]{1,0:T(1,128)}, f32[256,1152]{1,0:T(8,128)}, bf16[3,896,1152]{2,1,0:T(8,128)(2,1)}) custom-call(bf16[256,1152]{1,0:T(8,128)(2,1)} %get-tuple-element.77.own_rows, f32[256,1152]{1,0:T(8,128)} %get-tuple-element.78.middle_ref.middle_hbm, ...), custom_call_target="tpu_custom_call" | custom-call | flops 38050725888 | bytes 18579456 | tf_op jit(solution)/shard_map/pallas_call | solution.py:522
  215.0 105.3 %shard_map.405 = (bf16[3,224,1152]{2,1,0:T(8,128)(2,1)}, bf16[3,224,1152]{2,1,0:T(8,128)(2,1)}, bf16[160,1536]{1,0:T(8,128)(2,1)}, bf16[128,1152]{1,0:T(8,128)(2...) custom-call(f32[256,1152]{1,0:T(8,128)} %get-tuple-element.82.back_hbm, ...), custom_call_target="tpu_custom_call" | custom-call | flops 7247757312 | bytes 12386304 | tf_op jit(solution)/shard_map/pallas_call | solution.py:1221
  320.3 1.0 collective-permute-start
  321.3 1.0 collective-permute-start.1
  322.3 0.7 slice.7
  323.0 0.6 broadcast_subtract_fusion
  323.7 0.0 copy-start.8
  323.7 0.0 copy-start.9
  323.7 0.0 copy-start.10
  323.7 0.0 copy-start.1
  323.7 0.0 copy-start.7
  323.7 19.4 %shard_map.406 = (f32[864,1152]{1,0:T(8,128)}, f32[864,1152]{1,0:T(8,128)}, f32[864,1152]{1,0:T(8,128)}, f32[864,1152]{1,0:T(8,128)}, bf16[864,1152]{1,0:T(8,128...) custom-call(s32[2]{0:T(128)} %get-tuple-element.143.which, ...), custom_call_target="tpu_custom_call" | custom-call | flops 24772608 | bytes 49545216 | tf_op jit(solution)/shard_map/pallas_call | solution.py:1952
  343.1 0.0 copy-start
  343.1 0.0 copy-start.4
  343.1 0.0 copy-start.5
  343.1 0.0 copy-start.6
  343.2 0.0 copy-done.8
  343.2 0.0 copy-done.9
  343.2 0.0 copy-done.10
  343.2 0.7 fusion.3
  343.9 0.0 copy-done.1
  343.9 0.0 copy-done.7
  343.9 3.0 fusion.5
  346.9 0.0 copy-done
  346.9 0.0 copy-done.4
  346.9 0.0 copy-done.5
  346.9 0.0 copy-done.6
  347.0 2.2 fusion.7
  349.2 1.9 collective-permute-done.first_half
  351.1 0.0 copy-start.2
  351.1 0.6 collective-permute-done.1.second_half
  351.7 0.0 copy-start.3
  351.7 0.5 copy-done.2
  352.2 0.6 copy-done.3
  352.8 18.5 %shard_map.407 = (f32[864,1152]{1,0:T(8,128)}, f32[864,1152]{1,0:T(8,128)}, f32[864,1152]{1,0:T(8,128)}, f32[864,1152]{1,0:T(8,128)}, bf16[864,1152]{1,0:T(8,128...) custom-call(s32[2]{0:T(128)} %get-tuple-element.142.which, ...), custom_call_target="tpu_custom_call", output_to_operand_aliasing={{0}: (9, {}), {1}: (10, {}), {2}: (11, {}), {3}: (12, {}), ... | custom-call | flops 24772608 | bytes 49545216 | tf_op jit(solution)/shard_map/pallas_call | solution.py:1952
  (1 shorter events, 0.0 us)
Async XLA Ops:
  320.3 30.7 %collective-permute-start = (bf16[3,224,1152]{2,1,0:T(8,128)(2,1)}, bf16[3,224,1152]{2,1,0:T(8,128)(2,1)S(1)}, u32[]{:S(2)}, u32[]{:S(2)}) collective-permute-start(bf16[3,224,1152]{2,1,0:T(8,128)(2,1)} %get-tuple-element.99.first_half), channel_id=1, source_target_pairs={{0,8},{8,0},{16,24},{24,16},{1,9},{9,1},{17,25},{25,17},{2,10},{10... | collective-permute-start | bytes 4644872 | tf_op jit(solution)/shard_map/ppermute | solution.py:2139
  321.3 30.3 %collective-permute-start.1 = (bf16[3,224,1152]{2,1,0:T(8,128)(2,1)}, bf16[3,224,1152]{2,1,0:T(8,128)(2,1)S(1)}, u32[]{:S(2)}, u32[]{:S(2)}) collective-permute-start(bf16[3,224,1152]{2,1,0:T(8,128)(2,1)} %get-tuple-element.100.second_half), channel_id=1, source_target_pairs={{0,16},{8,24},{16,0},{24,8},{1,17},{9,25},{17,1},{25,9},{2,18},{10... | collective-permute-start | bytes 4644872 | tf_op jit(solution)/shard_map/ppermute | solution.py:2139
  323.7 19.5 %copy-start.8 = (f32[4,144]{1,0:T(4,128)S(1)}, f32[4,144]{1,0:T(4,128)}, u32[]{:S(2)}) copy-start(f32[4,144]{1,0:T(4,128)} %gains_in.1) | copy-start | bytes 6916
  323.7 19.5 %copy-start.9 = (f32[4,144]{1,0:T(4,128)S(1)}, f32[4,144]{1,0:T(4,128)}, u32[]{:S(2)}) copy-start(f32[4,144]{1,0:T(4,128)} %param.33) | copy-start | bytes 6916
  323.7 19.5 %copy-start.10 = (f32[4,144]{1,0:T(4,128)S(1)}, f32[4,144]{1,0:T(4,128)}, u32[]{:S(2)}) copy-start(f32[4,144]{1,0:T(4,128)} %param.38) | copy-start | bytes 6916
  323.7 20.2 %copy-start.1 = (f32[128,1152]{1,0:T(8,128)S(1)}, f32[128,1152]{1,0:T(8,128)}, u32[]{:S(2)}) copy-start(f32[128,1152]{1,0:T(8,128)} %out_in.1) | copy-start | bytes 1769476
  323.7 20.2 %copy-start.7 = (bf16[128,1152]{1,0:T(8,128)(2,1)S(1)}, bf16[128,1152]{1,0:T(8,128)(2,1)}, u32[]{:S(2)}) copy-start(bf16[128,1152]{1,0:T(8,128)(2,1)} %get-tuple-element.106) | copy-start | bytes 884740
  343.1 3.8 %copy-start = (f32[144,1536]{1,0:T(8,128)S(1)}, f32[144,1536]{1,0:T(8,128)}, u32[]{:S(2)}) copy-start(f32[144,1536]{1,0:T(8,128)} %qkv_in.1) | copy-start | bytes 2654212
  343.1 3.8 %copy-start.4 = (f32[144,1536]{1,0:T(8,128)S(1)}, f32[144,1536]{1,0:T(8,128)}, u32[]{:S(2)}) copy-start(f32[144,1536]{1,0:T(8,128)} %param.29) | copy-start | bytes 2654212
  343.1 3.8 %copy-start.5 = (f32[144,1536]{1,0:T(8,128)S(1)}, f32[144,1536]{1,0:T(8,128)}, u32[]{:S(2)}) copy-start(f32[144,1536]{1,0:T(8,128)} %param.34) | copy-start | bytes 2654212
  343.1 3.8 %copy-start.6 = (bf16[160,1536]{1,0:T(8,128)(2,1)S(1)}, bf16[160,1536]{1,0:T(8,128)(2,1)}, u32[]{:S(2)}) copy-start(bf16[160,1536]{1,0:T(8,128)(2,1)} %get-tuple-element.105) | copy-start | bytes 1474564
  351.1 1.1 copy-start.2
  351.7 1.2 copy-start.3
